TPU v7x, 32 devices: a whole 2x2x4 slice. The times are simulated.
32 devices in a mesh: cuts: 4 (over y, x), azim: 8 (over z, core).
Axes of the slice: x: 2, y: 2, z: 4, core: 2. Of those that a mesh axis runs over, the one named last changes fastest.
Arguments:
- potential: float32 [8, 1024, 4096], P('cuts', None, 'azim'), may hold values from -3 to 3
- direction: float32 [8, 1024, 4096], P('cuts', None, 'azim'), may hold values from -6 to 6
- source: float32 [8, 1024, 4096], P('cuts', None, 'azim'), may hold values from -6 to 6
- region_ids: int32 [8, 1024, 4096], P('cuts', None, 'azim'), may hold values from 0 to 7
- table_ids: int32 [8, 1024, 4096], P('cuts', None, 'azim'), may hold values from 0 to 15
- region_reluct: float32 [8], replicated, may hold values from 0.2 to 2
- table_sat: float32 [16], replicated, may hold values from 0.05 to 1
- skew_offsets: int32 [8], P('cuts'), may hold values from 0 to 4095
Outputs:
- residual: float32 [8, 1024, 4096], P('cuts', None, 'azim')
- jac_product: float32 [8, 1024, 4096], P('cuts', None, 'azim')
- gap_flux: float32 [2, 8, 2, 4096], P(None, 'cuts', None, 'azim')
Inputs may be any that keep to these rules, and one draw needn't show every extreme that they name: `region_ids`: each cell names one of the 8 material regions. `table_ids`: each cell names one of the 16 saturation entries.
All inputs are finite; a program needn't handle non-finite values.
Results may differ from a plain program's by a relative error of at most 0.000082.
Values sent between devices are 32-bit elements; how exact they have to be, the bound alone decides.
A program may use at most 192 MiB of HBM per device.

v0:
```python
import math

import jax
import jax.numpy as jnp
from jax import lax
from jax.sharding import PartitionSpec as P

R = 1024
P_SIZE = 4096
NREG = 8
NTAB = 16
M = 2048
RG = 512


GAP_SCALE = 4.0
highest = lax.Precision.HIGHEST


def with_halo(block, sides, width):
    for axis, dim in sides:
        count = lax.axis_size(axis)
        forward = [(i, i + 1) for i in range(count - 1)]
        forward.append((count - 1, 0))
        backward = [(target, source) for source, target in forward]
        low = lax.ppermute(
            lax.slice_in_dim(block, block.shape[dim] - width, None, axis=dim), axis, forward
        )
        high = lax.ppermute(lax.slice_in_dim(block, 0, width, axis=dim), axis, backward)
        block = jnp.concatenate([low, block, high], axis=dim)
    return block


def mode_table(col_start, col_count):
    columns = col_start + jnp.arange(col_count, dtype=jnp.int32)
    mode_ids = jnp.arange(M, dtype=jnp.int32)
    turns = (2 * mode_ids + 1)[None, :] * (2 * columns + 1)[:, None] % (4 * P_SIZE)
    phases = turns.astype(jnp.float32) * (math.pi / (2 * P_SIZE))
    return jnp.concatenate([jnp.cos(phases), jnp.sin(phases)], axis=1)


def mode_gains(mode_ids):
    wave = GAP_SCALE * (2 * mode_ids + 1).astype(jnp.float32) / (2 * M)
    return (wave / jnp.tanh(wave), wave / jnp.sinh(wave))


def skew_phases(offsets, mode_ids):
    turns = (2 * mode_ids + 1)[None, :] * offsets[:, None] % (2 * P_SIZE)
    phases = turns.astype(jnp.float32) * (math.pi / P_SIZE)
    return (jnp.cos(phases), jnp.sin(phases))


def axial_sum(total):
    return lax.psum(total, "cuts")


def couple(harmonics, offsets, mode_ids, slice_total):
    self_gain, cross_gain = mode_gains(mode_ids)
    cos_skew, sin_skew = skew_phases(offsets, mode_ids)
    cos_skew = cos_skew[None]
    sin_skew = sin_skew[None]
    rotor = harmonics[:, :, 0]
    stator = harmonics[:, :, 1]
    seen_c = stator[:, :, 0] * cos_skew + stator[:, :, 1] * sin_skew
    seen_s = stator[:, :, 1] * cos_skew - stator[:, :, 0] * sin_skew
    seen = jnp.stack([seen_c, seen_s], axis=2)
    axial = axial_sum(jnp.sum(seen, axis=1)) / slice_total
    blended = 0.5 * (seen + axial[:, None])
    rotor_flux = self_gain * rotor - cross_gain * blended
    back = self_gain * seen - cross_gain * rotor
    stator_c = back[:, :, 0] * cos_skew - back[:, :, 1] * sin_skew
    stator_s = back[:, :, 0] * sin_skew + back[:, :, 1] * cos_skew
    stator_flux = jnp.stack([stator_c, stator_s], axis=2)
    return jnp.stack([rotor_flux, stator_flux], axis=2)


def radial_diff(field, keep):
    inner = field[..., 1:, :] - field[..., :-1, :]
    return jnp.concatenate([inner, -field[..., -1:, :]], axis=-2) * keep


def cell_reluct(pot, pot_next, dirv, dir_next, base, satur, keep):
    rad_p = radial_diff(pot, keep)
    rad_d = radial_diff(dirv, keep)
    azi_p = pot_next - pot
    azi_d = dir_next - dirv
    square = rad_p * rad_p + azi_p * azi_p
    nu_val = base * (1.0 + satur * square)
    dnu_val = 2.0 * base * satur * (rad_p * rad_d + azi_p * azi_d)
    return (nu_val, dnu_val, (rad_p, rad_d, azi_p, azi_d))


def face_coeff(values, keep):
    inner = 0.5 * (values[..., :-1, :] + values[..., 1:, :])
    return jnp.concatenate([inner, values[..., -1:, :]], axis=-2) * keep


def neighbours(core, leading, trailing):
    column = lax.broadcasted_iota(jnp.int32, core.shape, core.ndim - 1)
    last_column = core.shape[-1] - 1
    following = jnp.where(column == last_column, trailing, jnp.roll(core, -1, axis=-1))
    preceding = jnp.where(column == 0, leading, jnp.roll(core, 1, axis=-1))
    return (following, preceding)


def cell_fluxes(
    pot,
    pot_prev,
    dirv,
    dir_prev,
    nu_val,
    nu_next,
    nu_prev,
    dnu_val,
    dnu_next,
    dnu_prev,
    diffs,
    keep,
    source,
):
    rad_p, rad_d, azi_p, azi_d = diffs
    back_p = pot - pot_prev
    back_d = dirv - dir_prev
    rad_k = face_coeff(nu_val, keep)
    rad_dk = face_coeff(dnu_val, keep)
    rad_f = rad_k * rad_p
    rad_df = rad_k * rad_d + rad_dk * rad_p
    inner_f = nu_val[..., :1, :] * pot[..., :1, :]
    inner_df = nu_val[..., :1, :] * dirv[..., :1, :] + dnu_val[..., :1, :] * pot[..., :1, :]
    radial = -(rad_f - jnp.concatenate([inner_f, rad_f[..., :-1, :]], axis=-2))
    radial_d = -(rad_df - jnp.concatenate([inner_df, rad_df[..., :-1, :]], axis=-2))
    fwd_k = 0.5 * (nu_val + nu_next)
    bwd_k = 0.5 * (nu_prev + nu_val)
    fwd_dk = 0.5 * (dnu_val + dnu_next)
    bwd_dk = 0.5 * (dnu_prev + dnu_val)
    azim = -(fwd_k * azi_p - bwd_k * back_p)
    azim_d = -(fwd_k * azi_d + fwd_dk * azi_p - (bwd_k * back_d + bwd_dk * back_p))
    return (radial + azim - source, radial_d + azim_d)


def lookup(ids, values, count):
    total = jnp.zeros(ids.shape, jnp.float32)
    for number in range(count):
        total = total + jnp.where(ids == number, values[number], 0.0)
    return total


def body(
    potential, direction, source, region_ids, table_ids, region_reluct, table_sat, skew_offsets
):
    position = lax.axis_index("azim")
    azim_count = lax.axis_size("azim")
    width = potential.shape[-1]
    slice_count = potential.shape[0]
    total_slices = slice_count * lax.axis_size("cuts")
    keep = (jnp.arange(R) != RG - 1).astype(jnp.float32)[:, None]
    table = mode_table(position * width, width)
    rows = jnp.stack([potential[:, RG - 1 : RG + 1, :], direction[:, RG - 1 : RG + 1, :]])
    partial_sums = jnp.dot(rows.reshape(-1, width), table, precision=highest).reshape(
        2, slice_count, 2, 2, M
    )
    harmonics = lax.psum(partial_sums, "azim")
    coupled = couple(harmonics, skew_offsets, jnp.arange(M, dtype=jnp.int32), total_slices)
    gap_flux = (
        jnp.dot(coupled.reshape(-1, 2 * M), table.T, precision=highest) * (2.0 / P_SIZE)
    ).reshape(2, slice_count, 2, width)
    left_sign = jnp.where(position == 0, -1.0, 1.0).astype(jnp.float32)
    right_sign = jnp.where(position == azim_count - 1, -1.0, 1.0).astype(jnp.float32)
    base = lookup(region_ids, region_reluct, NREG)
    satur = lookup(table_ids, table_sat, NTAB)
    fields = jnp.stack([potential, direction])
    edges = jnp.concatenate([fields[..., :1], fields[..., -1:]], axis=3)
    outer = with_halo(edges, (("azim", 3),), 1)
    before = outer[..., 0:1] * left_sign
    beyond = outer[..., 3:4] * right_sign
    pot_next, pot_prev = neighbours(potential, before[0], beyond[0])
    dir_next, dir_prev = neighbours(direction, before[1], beyond[1])
    nu_val, dnu_val, diffs = cell_reluct(
        potential, pot_next, direction, dir_next, base, satur, keep
    )
    reluct_edges = jnp.stack(
        [
            jnp.concatenate([nu_val[..., :1], nu_val[..., -1:]], axis=-1),
            jnp.concatenate([dnu_val[..., :1], dnu_val[..., -1:]], axis=-1),
        ]
    )
    reluct_outer = with_halo(reluct_edges, (("azim", 3),), 1)
    nu_left, nu_right = (reluct_outer[0, ..., 0:1], reluct_outer[0, ..., 3:4])
    dnu_left, dnu_right = (reluct_outer[1, ..., 0:1], reluct_outer[1, ..., 3:4])
    nu_next, nu_prev = neighbours(nu_val, nu_left, nu_right)
    dnu_next, dnu_prev = neighbours(dnu_val, dnu_left, dnu_right)
    residual, jac_product = cell_fluxes(
        potential,
        pot_prev,
        direction,
        dir_prev,
        nu_val,
        nu_next,
        nu_prev,
        dnu_val,
        dnu_next,
        dnu_prev,
        diffs,
        keep,
        source,
    )
    residual = residual.at[:, RG - 1 : RG + 1, :].add(gap_flux[0])
    jac_product = jac_product.at[:, RG - 1 : RG + 1, :].add(gap_flux[1])
    return (residual, jac_product, gap_flux)


def solution(mesh):
    return jax.shard_map(
        body,
        mesh=mesh,
        in_specs=(
            P("cuts", None, "azim"),
            P("cuts", None, "azim"),
            P("cuts", None, "azim"),
            P("cuts", None, "azim"),
            P("cuts", None, "azim"),
            P(),
            P(),
            P("cuts"),
        ),
        out_specs=(P("cuts", None, "azim"), P("cuts", None, "azim"), P(None, "cuts", None, "azim")),
        check_vma=False,
    )
```

profile of v0, /device:TPU:0, one launch (start us, length us, event | category | flops | bytes accessed | tf_op | source)
XLA Modules:
  0.0 421.0 jit_solution(18129519871088711707)
XLA Ops:
  7.2 7.3 %copy.164 = f32[2,1024,512]{1,0,2:T(2,128)} copy(f32[2,1024,512]{2,1,0:T(8,128)} %param.12) | data formatting | bytes 8388608 | tf_op args[0]
  14.5 7.3 %copy.165 = f32[2,1024,512]{1,0,2:T(2,128)} copy(f32[2,1024,512]{2,1,0:T(8,128)} %param.13) | data formatting | bytes 8388608 | tf_op args[1]
  22.6 4.5 %collective-permute-start = (f32[2,2,1024,1]{2,1,3,0:T(2,128)S(1)}, f32[2,2,1024,1]{2,1,3,0:T(2,128)S(1)}, u32[]{:S(2)}, u32[]{:S(2)}) collective-permute-start(f32[2,2,1024,1]{2,1,3,0:T(2,128)S(1)} %get-tuple-element.44), channel_id=1, source_target_pairs={{1,0},{2,1},{3,2},{4,3},{5,4},{6,5},{7,6},{0,7},{9,8},{10,9},{11,1... | collective-permute-start | bytes 49160 | tf_op jit(solution)/shard_map/ppermute | solution.py:29
  28.0 16.5 %fusion.53 = (f32[512,2048]{0,1:T(8,128)S(1)}, f32[512,2048]{0,1:T(8,128)S(1)}) fusion(s32[512]{0:T(512)S(1)} %multiply_add_fusion.3, s32[2048]{0:T(1024)S(1)} %multiply_add_fusion.2), kind=kLoop, calls=%fused_computation.103 | loop fusion | flops 14680064 | bytes 8398848 | tf_op jit(solution)/shard_map/cos | solution.py:39
  44.5 4.7 %pad_maximum_fusion = f32[512,4096]{0,1:T(8,128)} fusion(f32[512,2048]{0,1:T(8,128)S(1)} %get-tuple-element.84, f32[512,2048]{0,1:T(8,128)S(1)} %get-tuple-element.83), kind=kLoop, calls=%fused_computation | loop fusion | flops 2097152 | bytes 16777216 | tf_op jit(solution)/shard_map/concatenate | solution.py:39
  50.3 10.2 %fusion.62 = f32[2,2,2,2,2048]{4,2,3,1,0:T(2,128)} fusion(f32[2,2048,512,1,1]{2,1,0,4,3:T(8,128)} %bitcast.78, f32[1,2,2,512]{3,2,1,0:T(2,128)S(1)} %get-tuple-element.121, f32[1,2,2,512]{3,2,1,0:T(2,128)S(1)} %get-tuple-element.122), kind=kOutput, calls=%fused_computation.135 | convolution fusion | flops 201330688 | bytes 8536064 | tf_op jit(solution)/shard_map/dot_general | solution.py:159
  60.6 5.6 %copy.161 = f32[2,1024,512]{2,0,1:T(2,128)S(1)} copy(f32[2,1024,512]{2,1,0:T(8,128)} %param.12) | data formatting | bytes 8388608 | tf_op args[0]
  69.4 13.6 %fusion.80 = (f32[2,1024,511]{2,0,1:T(2,128)}, f32[2,1024,511]{2,0,1:T(2,128)}, f32[2,1024,511]{2,0,1:T(2,128)}, f32[2,1024,511]{2,0,1:T(2,128)}) fusion(f32[2,1024,512]{2,0,1:T(2,128)S(1)} %copy.173, f32[2,1024,512]{2,0,1:T(2,128)S(1)} %copy.161), kind=kLoop, calls=%fused_computation.181 | loop fusion | bytes 33488896 | tf_op jit(solution)/shard_map/jit(_roll_static)/slice | solution.py:102
  87.2 6.3 %slice_subtract_fusion = (f32[2,1023,512]{2,0,1:T(2,128)}, f32[2,1023,512]{2,0,1:T(2,128)}) fusion(f32[2,1024,512]{2,0,1:T(2,128)S(1)} %copy.173, f32[2,1024,512]{2,0,1:T(2,128)S(1)} %copy.161), kind=kLoop, calls=%fused_computation.98 | loop fusion | flops 2095104 | bytes 25141248 | tf_op jit(solution)/shard_map/sub | solution.py:78
  96.0 78.5 %add_multiply_fusion = (f32[2,1024,512]{2,0,1:T(2,128)S(1)}, f32[2,1024,512]{2,0,1:T(2,128)S(1)}, f32[2,1024,512]{2,0,1:T(2,128)S(1)}) fusion(f32[2,1024,1]{2,0,1:T(2,128)S(1)} %get-tuple-element.48, f32[2,1024,511]{2,0,1:T(2,128)} %get-tuple-element.50, f32[2,1024]{0,1:T(8,128)S(1)} %copy.176, pred[512]{0:T(512)(128)(4,1)S(1)} %get-tuple-element.120, ...), kind=kLoop, calls=%fused_computation.94 | loop fusion | flops 90177536 | bytes 46158432 | tf_op jit(solution)/shard_map/mul | solution.py:89
  174.6 28.8 %add_multiply_fusion.1 = f32[2,1024,512]{2,0,1:T(2,128)S(1)} fusion(f32[2,1024,512]{2,0,1:T(2,128)S(1)} %get-tuple-element.38, f32[2,1024,512]{2,0,1:T(2,128)S(1)} %get-tuple-element.37, f32[]{:T(128)} %bitcast.7, f32[]{:T(128)} %bitcast.6, f32[]{:T(128)} %bitcast.5, f32[]{:T(128)} %bitcast.4, f32[]{:T(128)} %bitcast.3, f32[]{:T(128)} %bitcast.2, ...), kind=kLoop, calls=%fused_computation.95 | loop fusion | flops 32505856 | bytes 20975648 | tf_op jit(solution)/shard_map/mul | solution.py:88
  204.8 5.4 %fusion.51 = f32[2,1023,512]{2,0,1:T(2,128)} fusion(f32[2,1024,512]{2,0,1:T(2,128)S(1)} %add_multiply_fusion.1), kind=kLoop, calls=%fused_computation.100 | loop fusion | flops 2095104 | bytes 12570624 | tf_op jit(solution)/shard_map/mul | solution.py:94
  213.6 5.4 %fusion.50 = f32[2,1023,512]{2,0,1:T(2,128)} fusion(f32[2,1024,512]{2,0,1:T(2,128)S(1)} %get-tuple-element.36), kind=kLoop, calls=%fused_computation.97 | loop fusion | flops 2095104 | bytes 12570624 | tf_op jit(solution)/shard_map/mul | solution.py:94
  219.0 9.2 %fusion.81 = (f32[2,1024,511]{2,0,1:T(2,128)}, f32[2,1024,511]{2,0,1:T(2,128)}) fusion(f32[2,1024,512]{2,0,1:T(2,128)S(1)} %add_multiply_fusion.1), kind=kLoop, calls=%fused_computation.182 | loop fusion | bytes 16744448 | tf_op jit(solution)/shard_map/jit(_roll_static)/slice | solution.py:101
  235.7 21.9 %fusion.36 = (f32[2,1024,512]{2,0,1:T(2,128)}, f32[2,1024,512]{2,0,1:T(2,128)}) fusion(f32[2,1,512]{2,0,1:T(2,128)S(1)} %get-tuple-element.52, f32[2,1023,512]{2,0,1:T(2,128)} %fusion.50, f32[1024]{0:T(1024)S(1)} %fusion.73, f32[2,1,512]{2,0,1:T(2,128)S(1)} %get-tuple-element.113, f32[2,1023,512]{2,0,1:T(2,128)} %get-tuple-element.111, ...), kind=kLoop, calls=%fused_computation.76 | loop fusion | flops 12582912 | bytes 25169920 | tf_op jit(solution)/shard_map/add | solution.py:127
  257.6 9.1 %fusion.78 = (f32[2,1024,511]{2,0,1:T(2,128)}, f32[2,1024,511]{2,0,1:T(2,128)}) fusion(f32[2,1024,512]{2,0,1:T(2,128)S(1)} %copy-done.3), kind=kLoop, calls=%fused_computation.179 | loop fusion | bytes 16744448 | tf_op jit(solution)/shard_map/jit(_roll_static)/slice | solution.py:101
  266.7 5.6 %slice.430 = f32[2,1023,512]{2,0,1:T(2,128)} slice(f32[2,1024,512]{2,0,1:T(2,128)} %get-tuple-element.39), slice={[0:2], [0:1023], [0:512]} | slice | bytes 8380416 | tf_op jit(solution)/shard_map/slice | solution.py:131
  274.4 5.7 %slice.397 = f32[2,1023,512]{2,0,1:T(2,128)} slice(f32[2,1024,512]{2,0,1:T(2,128)} %get-tuple-element.40), slice={[0:2], [0:1023], [0:512]} | slice | bytes 8380416 | tf_op jit(solution)/shard_map/slice | solution.py:130
  284.3 61.3 %fusion.38 = f32[2,1024,512]{2,0,1:T(2,128)} fusion(f32[2,1024,512]{2,0,1:T(2,128)} %get-tuple-element.39, f32[2,1023,512]{2,0,1:T(2,128)} %slice.430, f32[2,1,512]{2,0,1:T(2,128)S(1)} %get-tuple-element.41, f32[2,1024,512]{2,0,1:T(2,128)} %copy-done.2, f32[2,1024,511]{2,0,1:T(2,128)} %get-tuple-element.46, f32[2,1024,1]{2,0,1:T(2,128)} %get-tuple-element.58, ...), kind=kLoop, calls=%fused_computation.79 | loop fusion | flops 38797312 | bytes 62972928 | tf_op jit(solution)/shard_map/add | solution.py:138
  345.7 30.9 %fusion.28 = f32[2,1024,512]{2,0,1:T(2,128)} fusion(f32[2,1024,512]{2,0,1:T(2,128)} %get-tuple-element.40, f32[2,1023,512]{2,0,1:T(2,128)} %slice.397, f32[2,1,512]{2,0,1:T(2,128)S(1)} %get-tuple-element.42, f32[2,1024,512]{2,1,0:T(8,128)} %param.14, f32[2,1024,512]{2,0,1:T(2,128)S(1)} %copy-done.9, f32[2,1024,511]{2,0,1:T(2,128)S(1)} %copy-done.15, ...), kind=kLoop, calls=%fused_computation.62 | loop fusion | flops 20971520 | bytes 41968640 | tf_op jit(solution)/shard_map/sub | solution.py:138
  378.0 16.3 %psum.15 = f32[2,2,2048]{2,1,0:T(2,128)S(1)} all-reduce(f32[2,2,2048]{2,1,0:T(2,128)S(1)} %get-tuple-element.69), channel_id=1, replica_groups=mesh['cuts'=4,'azim'=8] {'cuts'}, use_global_device_ids=true, to_apply=%region_2.3 | all-reduce | flops 8192 | bytes 65536 | tf_op jit(solution)/shard_map/psum | solution.py:54
  394.7 5.7 %convolution_multiply_fusion = f32[8,512]{1,0:T(8,128)S(1)} fusion(f32[8,4096]{1,0:T(8,128)S(1)} %bitcast.81, f32[512,2048]{0,1:T(8,128)} %copy-done.14, f32[512,2048]{0,1:T(8,128)} %copy-done.13), kind=kOutput, calls=%fused_computation.104 | convolution fusion | flops 203427840 | bytes 8536064 | tf_op jit(solution)/shard_map/dot_general | solution.py:165
  402.4 5.0 %copy.203 = f32[2,1024,512]{2,1,0:T(8,128)} copy(f32[2,1024,512]{2,0,1:T(2,128)} %fusion.68) | data formatting | bytes 8388608
  408.7 5.0 %copy.202 = f32[2,1024,512]{2,1,0:T(8,128)} copy(f32[2,1024,512]{2,0,1:T(2,128)} %fusion.69) | data formatting | bytes 8388608
  (117 shorter events, 36.2 us)
Async XLA Ops:
  7.2 369.4 %all-reduce.2.cloned.1.call-start = ((), (), s32[]{:S(2)}) async-start(), calls=%async_computation | async-start | bytes 262144 | tf_op jit(solution)/shard_map/psum | solution.py:162
  22.6 72.9 %collective-permute-start = (f32[2,2,1024,1]{2,1,3,0:T(2,128)S(1)}, f32[2,2,1024,1]{2,1,3,0:T(2,128)S(1)}, u32[]{:S(2)}, u32[]{:S(2)}) collective-permute-start(f32[2,2,1024,1]{2,1,3,0:T(2,128)S(1)} %get-tuple-element.44), channel_id=1, source_target_pairs={{1,0},{2,1},{3,2},{4,3},{5,4},{6,5},{7,6},{0,7},{9,8},{10,9},{11,1... | collective-permute-start | bytes 49160 | tf_op jit(solution)/shard_map/ppermute | solution.py:29
  27.1 239.6 %collective-permute-start.3 = (f32[2,2,1024,1]{2,1,3,0:T(2,128)S(1)}, f32[2,2,1024,1]{2,1,3,0:T(2,128)S(1)}, u32[]{:S(2)}, u32[]{:S(2)}) collective-permute-start(f32[2,2,1024,1]{2,1,3,0:T(2,128)S(1)} %get-tuple-element.43), channel_id=1, source_target_pairs={{0,1},{1,2},{2,3},{3,4},{4,5},{5,6},{6,7},{7,0},{8,9},{9,10},{10,1... | collective-permute-start | bytes 49160 | tf_op jit(solution)/shard_map/ppermute | solution.py:26
  66.2 27.4 %copy-start.4 = (f32[2,1024,512]{2,0,1:T(2,128)}, f32[2,1024,512]{2,0,1:T(2,128)S(1)}, u32[]{:S(2)}) copy-start(f32[2,1024,512]{2,0,1:T(2,128)S(1)} %copy.161) | copy-start | bytes 12582916
  69.4 24.2 %copy-start.5 = (f32[2,1024,512]{2,0,1:T(2,128)}, f32[2,1024,512]{2,0,1:T(2,128)S(1)}, u32[]{:S(2)}) copy-start(f32[2,1024,512]{2,0,1:T(2,128)S(1)} %copy.173) | copy-start | bytes 12582916
  87.2 8.7 %copy-start.19 = (f32[2,1024,1]{2,0,1:T(2,128)}, f32[2,1024,1]{2,0,1:T(2,128)S(1)}, u32[]{:S(2)}) copy-start(f32[2,1024,1]{2,0,1:T(2,128)S(1)} %get-tuple-element.48) | copy-start | bytes 24580
  95.7 78.8 %copy-start.20 = (f32[2,1024]{0,1:T(8,128)}, f32[2,1024]{0,1:T(8,128)S(1)}, u32[]{:S(2)}) copy-start(f32[2,1024]{0,1:T(8,128)S(1)} %copy.176) | copy-start | bytes 24580
  95.9 78.6 %copy-start.10 = (f32[2,1023,512]{2,0,1:T(2,128)S(1)}, f32[2,1023,512]{2,0,1:T(2,128)}, u32[]{:S(2)}) copy-start(f32[2,1023,512]{2,0,1:T(2,128)} %get-tuple-element.112) | copy-start | bytes 12570628
  96.0 78.6 %copy-start.18 = (s32[2,1024,512]{2,1,0:T(8,128)S(1)}, s32[2,1024,512]{2,1,0:T(8,128)}, u32[]{:S(2)}) copy-start(s32[2,1024,512]{2,1,0:T(8,128)} %param.15) | copy-start | bytes 12582916
  174.5 28.8 %copy-start.8 = (f32[2,1024,512]{2,0,1:T(2,128)}, f32[2,1024,512]{2,0,1:T(2,128)S(1)}, u32[]{:S(2)}) copy-start(f32[2,1024,512]{2,0,1:T(2,128)S(1)} %get-tuple-element.37) | copy-start | bytes 12582916
  174.5 39.0 %copy-start.2 = (f32[2,1024,512]{2,0,1:T(2,128)}, f32[2,1024,512]{2,0,1:T(2,128)S(1)}, u32[]{:S(2)}) copy-start(f32[2,1024,512]{2,0,1:T(2,128)S(1)} %get-tuple-element.36) | copy-start | bytes 12582916
  203.3 15.6 %copy-start = (f32[2,1024,512]{2,0,1:T(2,128)}, f32[2,1024,512]{2,0,1:T(2,128)S(1)}, u32[]{:S(2)}) copy-start(f32[2,1024,512]{2,0,1:T(2,128)S(1)} %add_multiply_fusion.1) | copy-start | bytes 12582916
  204.8 26.2 %copy-start.16 = (f32[2,1024,1]{2,0,1:T(2,128)}, f32[2,1024,1]{2,0,1:T(2,128)S(1)}, u32[]{:S(2)}) copy-start(f32[2,1024,1]{2,0,1:T(2,128)S(1)} %get-tuple-element.55) | copy-start | bytes 24580
  204.8 26.7 %copy-start.17 = (f32[2,1024,1]{2,0,1:T(2,128)}, f32[2,1024,1]{2,0,1:T(2,128)S(1)}, u32[]{:S(2)}) copy-start(f32[2,1024,1]{2,0,1:T(2,128)S(1)} %get-tuple-element.56) | copy-start | bytes 24580
  232.1 48.0 %collective-permute-start.1 = (f32[2,2,1024,1]{2,1,3,0:T(2,128)S(1)}, f32[2,2,1024,1]{2,1,3,0:T(2,128)S(1)}, u32[]{:S(2)}, u32[]{:S(2)}) collective-permute-start(f32[2,2,1024,1]{2,1,3,0:T(2,128)S(1)} %copy.207), channel_id=1, source_target_pairs={{1,0},{2,1},{3,2},{4,3},{5,4},{6,5},{7,6},{0,7},{9,8},{10,9},{11,1... | collective-permute-start | bytes 49160 | tf_op jit(solution)/shard_map/ppermute | solution.py:29
  235.7 45.5 %collective-permute-start.2 = (f32[2,2,1024,1]{2,1,3,0:T(2,128)S(1)}, f32[2,2,1024,1]{2,1,3,0:T(2,128)S(1)}, u32[]{:S(2)}, u32[]{:S(2)}) collective-permute-start(f32[2,2,1024,1]{2,1,3,0:T(2,128)S(1)} %copy.208), channel_id=1, source_target_pairs={{0,1},{1,2},{2,3},{3,4},{4,5},{5,6},{6,7},{7,0},{8,9},{9,10},{10,1... | collective-permute-start | bytes 49160 | tf_op jit(solution)/shard_map/ppermute | solution.py:26
  235.7 21.9 %copy-start.3 = (f32[2,1024,512]{2,0,1:T(2,128)S(1)}, f32[2,1024,512]{2,0,1:T(2,128)}, u32[]{:S(2)}) copy-start(f32[2,1024,512]{2,0,1:T(2,128)} %copy-done.2) | copy-start | bytes 12582916
  274.4 9.8 %copy-start.21 = (f32[2,1024]{0,1:T(8,128)S(1)}, f32[2,1024]{0,1:T(8,128)}, u32[]{:S(2)}) copy-start(f32[2,1024]{0,1:T(8,128)} %copy-done.20) | copy-start | bytes 24580
  284.2 61.4 %copy-start.1 = (f32[2,1024,512]{2,0,1:T(2,128)S(1)}, f32[2,1024,512]{2,0,1:T(2,128)}, u32[]{:S(2)}) copy-start(f32[2,1024,512]{2,0,1:T(2,128)} %copy-done) | copy-start | bytes 12582916
  284.3 61.4 %copy-start.6 = (f32[2,1024,512]{2,1,0:T(8,128)S(1)}, f32[2,1024,512]{2,1,0:T(8,128)}, u32[]{:S(2)}) copy-start(f32[2,1024,512]{2,1,0:T(8,128)} %param.12) | copy-start | bytes 12582916
  284.3 61.4 %copy-start.9 = (f32[2,1024,512]{2,0,1:T(2,128)S(1)}, f32[2,1024,512]{2,0,1:T(2,128)}, u32[]{:S(2)}) copy-start(f32[2,1024,512]{2,0,1:T(2,128)} %copy-done.8) | copy-start | bytes 12582916
  284.3 61.4 %copy-start.11 = (f32[2,1024,511]{2,0,1:T(2,128)S(1)}, f32[2,1024,511]{2,0,1:T(2,128)}, u32[]{:S(2)}) copy-start(f32[2,1024,511]{2,0,1:T(2,128)} %get-tuple-element.53) | copy-start | bytes 12558340
  284.3 61.4 %copy-start.12 = (f32[2,1024,511]{2,0,1:T(2,128)S(1)}, f32[2,1024,511]{2,0,1:T(2,128)}, u32[]{:S(2)}) copy-start(f32[2,1024,511]{2,0,1:T(2,128)} %get-tuple-element.54) | copy-start | bytes 12558340
  284.3 61.4 %copy-start.15 = (f32[2,1024,511]{2,0,1:T(2,128)S(1)}, f32[2,1024,511]{2,0,1:T(2,128)}, u32[]{:S(2)}) copy-start(f32[2,1024,511]{2,0,1:T(2,128)} %get-tuple-element.118) | copy-start | bytes 12558340
  (6 other events, 37.6 us)
Sparse Core Ops, SparseCore 0:
  60.7 55.4 all-reduce.1
where the time goes:
time: 430 us; the launch traced here: 421 us
  other arithmetic  265 us (62%)
  local copies, waits for them, and re-layouts  101 us (23%)
  blocking collectives  16.3 us (4%)
  matrix products  16 us (4%)
  between operations  15 us (3%)
  starting transfers between devices  8.23 us (2%)
    mul x1, other arithmetic, cell_reluct(): dnu_val = 2.0 * base * satur * (rad_p * rad_d + azi_p * azi_d)  78.5 us
    add x1, other arithmetic, cell_fluxes(): return (radial + azim - source, radial_d + azim_d)  61.3 us
    unnamed x60, local copies, waits for them, and re-layouts  34.7 us
    sub x1, other arithmetic, cell_fluxes(): return (radial + azim - source, radial_d + azim_d)  30.9 us
    mul x1, other arithmetic, cell_reluct(): nu_val = base * (1.0 + satur * square)  28.8 us
    add x1, other arithmetic, cell_fluxes(): rad_df = rad_k * rad_d + rad_dk * rad_p  21.9 us
    slice x2, local copies, waits for them, and re-layouts, neighbours(): jnp.roll(core, -1, axis=-1)  18.2 us
    slice x2, local copies, waits for them, and re-layouts, neighbours(): preceding = jnp.where(column == 0, leading, jnp.roll(core, 1, axis=-1))  17.8 us
  transfers between devices with their start and end apart: 5, of which 0 were waited for; matrix products, arithmetic and copies ran while one was open for 82% of the time, Pallas kernels for 0%

commit v1 on v0

v1 whole, which is shorter than its diff:
```python
import functools
import math

import jax
import jax.numpy as jnp
import numpy as np
from jax import lax
from jax.experimental import pallas as pl
from jax.experimental.pallas import tpu as pltpu
from jax.sharding import PartitionSpec as P

NREG = 8
NTAB = 16
RG = 512
GAP_SCALE = 4.0
LANES = 128
highest = lax.Precision.HIGHEST


def transform_tables(period):
    ka = period // (2 * LANES)
    a = np.arange(ka)
    b = np.arange(LANES)
    first = np.exp(-2j * np.pi * np.outer(a, a) / ka - 1j * np.pi * a[None, :] * LANES / period)
    w1 = np.block([[first.real, first.imag], [first.imag, -first.real]])
    twiddle = np.exp(
        -2j * np.pi * np.outer(a, b) / (ka * LANES) - 1j * np.pi * b[None, :] / period
    )
    second = np.exp(-2j * np.pi * np.outer(b, b) / LANES)
    w2 = np.block([[second.real, second.imag], [-second.imag, second.real]])
    back2 = np.conj(second)
    w2i = np.block([[back2.real, back2.imag], [-back2.imag, back2.real]])
    back1 = np.conj(first).T / (ka * LANES)
    w1i = np.block([[back1.real, -back1.imag], [-back1.imag, -back1.real]])
    freq = (4 * (a[:, None] + ka * b[None, :]) + 1) % (2 * period)
    odd = np.minimum(freq, 2 * period - freq)
    wave = GAP_SCALE * odd / period
    gains = np.stack([wave / np.tanh(wave), wave / np.sinh(wave)])
    twiddles = np.stack([twiddle.real, twiddle.imag])
    return [np.asarray(t, np.float32) for t in (w1, twiddles, w2, w2i, w1i, gains)]


def edge_kernel(
    off_ref, af, al, vf, vl, rf, rl, tf, tl, a0, a1, v0, v1, left_ref, right_ref, rows_ref
):
    s = pl.program_id(0)
    rows = af.shape[1]
    lane = lax.broadcasted_iota(jnp.int32, (LANES, LANES), 1)
    last = LANES - 1

    def pick(mix, ref, at, source, target):
        tile = ref[0, pl.ds(at, LANES), :].astype(jnp.float32)
        shift = (target - source) % LANES
        if shift:
            tile = pltpu.roll(tile, shift, 1)
        return jnp.where(lane == target, tile, mix)

    for block in range(rows // LANES):
        at = block * LANES
        mix = jnp.zeros((LANES, LANES), jnp.float32)
        tile = af[0, pl.ds(at, LANES), :]
        mix = jnp.where(lane < 2, tile, mix)
        tile = pltpu.roll(vf[0, pl.ds(at, LANES), :], 2, 1)
        mix = jnp.where((lane >= 2) & (lane < 4), tile, mix)
        mix = pick(mix, rf, at, 0, 4)
        mix = pick(mix, tf, at, 0, 5)
        mix = pick(mix, al, at, last, 8)
        mix = pick(mix, vl, at, last, 9)
        mix = pick(mix, rl, at, last, 10)
        mix = pick(mix, tl, at, last, 11)
        flat = jnp.transpose(mix)
        left_ref[0, :, pl.ds(at, LANES)] = flat[0:8]
        right_ref[0, :, pl.ds(at, LANES)] = flat[8:16]
    count = rows_ref.shape[2]
    for c in range(count):
        cut = pl.ds(c * LANES, LANES)
        rows_ref[0, 0, c : c + 1, :] = a0[0, 7:8, cut]
        rows_ref[0, 1, c : c + 1, :] = a1[0, 0:1, cut]
        rows_ref[0, 2, c : c + 1, :] = v0[0, 7:8, cut]
        rows_ref[0, 3, c : c + 1, :] = v1[0, 0:1, cut]
        rows_ref[0, 4, c : c + 1, :] = jnp.full((1, LANES), off_ref[s], jnp.int32).astype(
            jnp.float32
        )


def edges(potential, direction, regions, tables, offsets):
    slices, rows, width = potential.shape
    count = width // LANES
    first = pl.BlockSpec((1, rows, LANES), lambda s: (s, 0, 0))
    last = pl.BlockSpec((1, rows, LANES), lambda s: (s, 0, count - 1))
    rotor = pl.BlockSpec((1, 8, width), lambda s: (s, RG // 8 - 1, 0))
    stator = pl.BlockSpec((1, 8, width), lambda s: (s, RG // 8, 0))
    return pl.pallas_call(
        edge_kernel,
        grid=(slices,),
        in_specs=[pl.BlockSpec(memory_space=pltpu.SMEM)]
        + [first, last] * 4
        + [rotor, stator] * 2,
        out_specs=[
            pl.BlockSpec((1, 8, rows), lambda s: (s, 0, 0)),
            pl.BlockSpec((1, 8, rows), lambda s: (s, 0, 0)),
            pl.BlockSpec((1, 5, count, LANES), lambda s: (s, 0, 0, 0)),
        ],
        out_shape=[
            jax.ShapeDtypeStruct((slices, 8, rows), jnp.float32),
            jax.ShapeDtypeStruct((slices, 8, rows), jnp.float32),
            jax.ShapeDtypeStruct((slices, 5, count, LANES), jnp.float32),
        ],
        compiler_params=pltpu.CompilerParams(vmem_limit_bytes=32 * 2**20),
        cost_estimate=pl.CostEstimate(
            flops=slices * rows * 1000, bytes_accessed=slices * rows * 4096, transcendentals=0
        ),
    )(
        offsets,
        potential,
        potential,
        direction,
        direction,
        regions,
        regions,
        tables,
        tables,
        potential,
        potential,
        direction,
        direction,
    )


def stencil_kernel(
    reg_s,
    tab_s,
    sign_s,
    regv,
    tabv,
    own_ref,
    low_ref,
    high_ref,
    a_ref,
    v_ref,
    src_ref,
    r_ref,
    t_ref,
    ax,
    vx,
    rx,
    tx,
    res_ref,
    jac_ref,
    halo,
    carry_ref,
):
    block = pl.program_id(1)
    blocks = pl.num_programs(1)
    size = a_ref.shape[1]
    count = a_ref.shape[2] // LANES
    rows = own_ref.shape[2]
    tiles = size // 8
    shape = (8, LANES)
    lane = lax.broadcasted_iota(jnp.int32, shape, 1)
    row = lax.broadcasted_iota(jnp.int32, shape, 0)
    at_end = lane == LANES - 1
    at_start = lane == 0
    at_bottom = row == 7
    at_top = row == 0
    reg_tab = jnp.broadcast_to(regv[0:1, :], shape)
    sat_tab = jnp.broadcast_to(tabv[0:1, :], shape)

    @pl.when(block == 0)
    def _():
        col = lax.broadcasted_iota(jnp.int32, (1, rows), 1)

        def pick(ids, table, number):
            total = jnp.zeros_like(ids)
            for i in range(number):
                total = jnp.where(ids == float(i), table[i], total)
            return total

        def material(a, a_next, v, v_next, reg, tab):
            def radial(x):
                follow = jnp.where(col == rows - 1, 0.0, pltpu.roll(x, rows - 1, 1))
                return jnp.where(col == RG - 1, 0.0, follow - x)

            base = pick(reg, reg_s, NREG)
            satur = pick(tab, tab_s, NTAB)
            rp, rd = radial(a), radial(v)
            zp, zd = a_next - a, v_next - v
            nu = base * (1.0 + satur * (rp * rp + zp * zp))
            dnu = 2.0 * base * satur * (rp * rd + zp * zd)
            return nu, dnu, zp, zd

        own = [own_ref[0, i : i + 1, :] for i in range(6)]
        high = [high_ref[0, i : i + 1, :] for i in range(6)]
        low = [low_ref[0, i : i + 1, :] for i in range(4)]
        ls, rs = sign_s[0], sign_s[1]
        high = [x * rs for x in high[:4]] + high[4:]
        low = [x * ls for x in low[:2]] + low[2:]
        nu0, dnu0, _, _ = material(*own)
        nur, dnur, _, _ = material(*high)
        nul, dnul, zp, zd = material(low[0], own[0], low[1], own[2], low[2], low[3])
        k = 0.5 * (nul + nu0)
        dk = 0.5 * (dnul + dnu0)
        flux = k * zp
        dflux = k * zd + dk * zp
        pack = jnp.concatenate(
            [flux, dflux, dflux, dflux, high[0], high[2], nur, dnur], axis=0
        )
        for i in range(rows // LANES):
            piece = jnp.concatenate(
                [
                    jnp.broadcast_to(pack[0:1, i * LANES : (i + 1) * LANES], (LANES - 8, LANES)),
                    pack[:, i * LANES : (i + 1) * LANES],
                ],
                axis=0,
            )
            halo[i * LANES : (i + 1) * LANES, :] = jnp.transpose(piece)


    def load(ref, at):
        return [ref[0, pl.ds(at, 8), c * LANES : (c + 1) * LANES] for c in range(count)]

    def up(x, follow):
        return [
            jnp.where(at_bottom, pltpu.roll(y, 7, 0), pltpu.roll(z, 7, 0))
            for z, y in zip(x, follow)
        ]

    def down(x, before):
        return [
            jnp.where(at_top, pltpu.roll(y, 1, 0), pltpu.roll(z, 1, 0))
            for z, y in zip(x, before)
        ]

    def forward(x, end):
        turned = [pltpu.roll(z, LANES - 1, 1) for z in x]
        return [
            jnp.where(at_end, turned[c + 1] if c + 1 < count else end, turned[c])
            for c in range(count)
        ]

    def backward(x, start):
        turned = [pltpu.roll(z, 1, 1) for z in x]
        return [jnp.where(at_start, turned[c - 1] if c else start, turned[c]) for c in range(count)]

    def each(f, *xs):
        return [f(*x) for x in zip(*xs)]

    def material(a, v, a_down, v_down, reg, tab, h):
        rp = each(lambda x, y: y - x, a, a_down)
        rd = each(lambda x, y: y - x, v, v_down)
        zp = each(lambda x, y: y - x, a, forward(a, pltpu.roll(h, 3, 1)))
        zd = each(lambda x, y: y - x, v, forward(v, pltpu.roll(h, 2, 1)))

        def coefficients(rp, rd, zp, zd, reg, tab):
            base = jnp.take_along_axis(reg_tab, reg, axis=1, mode="promise_in_bounds")
            satur = jnp.take_along_axis(sat_tab, tab, axis=1, mode="promise_in_bounds")
            bs = base * satur
            return (
                0.5 * (base + bs * (rp * rp + zp * zp)),
                bs * (rp * rd + zp * zd),
            )

        both = each(coefficients, rp, rd, zp, zd, reg, tab)
        return [x[0] for x in both], [x[1] for x in both], rp, rd, zp, zd

    start_row = block * size

    def halo_at(at):
        return halo[pl.ds(pl.multiple_of(start_row + at, 8), 8), :]

    def emit(at, cur, h, nu_next, dnu_next, fr_before, dfr_before):
        nu, dnu, rp, rd, zp, zd = cur
        kr = each(lambda x, y: x + y, nu, up(nu, nu_next))
        dkr = each(lambda x, y: x + y, dnu, up(dnu, dnu_next))
        fr = each(lambda x, y: x * y, kr, rp)
        dfr = each(lambda k, d, dk, p: k * d + dk * p, kr, rd, dkr, rp)
        half = 0.5
        kf = each(lambda x, y: x + y, nu, forward(nu, half * pltpu.roll(h, 1, 1)))
        dkf = each(lambda x, y: x + y, dnu, forward(dnu, half * h))
        fz = each(lambda x, y: x * y, kf, zp)
        dfz = each(lambda k, d, dk, p: k * d + dk * p, kf, zd, dkf, zp)
        fr_up = down(fr, fr_before)
        dfr_up = down(dfr, dfr_before)
        fz_back = backward(fz, h)
        dfz_back = backward(dfz, pltpu.roll(h, LANES - 121, 1))
        for c in range(count):
            cut = slice(c * LANES, (c + 1) * LANES)
            where = (0, pl.ds(at, 8), cut)
            res_ref[where] = (fr_up[c] - fr[c]) + (fz_back[c] - fz[c]) - src_ref[where]
            jac_ref[where] = (dfr_up[c] - dfr[c]) + (dfz_back[c] - dfz[c])
        return fr, dfr

    def tile_material(at, a_after, v_after):
        a, v = load(a_ref, at), load(v_ref, at)
        h = halo_at(at)
        return material(
            a, v, up(a, a_after), up(v, v_after), load(r_ref, at), load(t_ref, at), h
        )

    cur = tile_material(0, load(a_ref, 8), load(v_ref, 8))

    @pl.when(block == 0)
    def _():
        a, v = load(a_ref, 0), load(v_ref, 0)
        for c in range(count):
            cut = slice(c * LANES, (c + 1) * LANES)
            inner = 2.0 * cur[0][c] * a[c]
            dinner = 2.0 * cur[0][c] * v[c] + 2.0 * cur[1][c] * a[c]
            carry_ref[0, :, cut] = pltpu.roll(inner, 7, 0)
            carry_ref[1, :, cut] = pltpu.roll(dinner, 7, 0)

    fr = [carry_ref[0, :, c * LANES : (c + 1) * LANES] for c in range(count)]
    dfr = [carry_ref[1, :, c * LANES : (c + 1) * LANES] for c in range(count)]

    def step(t, state):
        cur, fr, dfr = state
        at = pl.multiple_of(t * 8, 8)
        after = pl.multiple_of(t * 8 + 8, 8)
        beyond = pl.multiple_of(t * 8 + 16, 8)
        following = tile_material(after, load(a_ref, beyond), load(v_ref, beyond))
        fr, dfr = emit(at, cur, halo_at(at), following[0], following[1], fr, dfr)
        return following, fr, dfr

    cur, fr, dfr = lax.fori_loop(0, tiles - 2, step, (cur, fr, dfr))

    is_last = block == blocks - 1
    is_gap = start_row + size == RG
    end = size - 8

    def ending(ref, ext):
        own, beyond = load(ref, end), load(ext, 0)
        return each(
            lambda x, y: jnp.where(is_gap, pltpu.roll(x, 1, 0), jnp.where(is_last, 0.0, y)),
            own,
            beyond,
        )

    following = tile_material(end, ending(a_ref, ax), ending(v_ref, vx))
    fr, dfr = emit(end - 8, cur, halo_at(end - 8), following[0], following[1], fr, dfr)
    cur = following
    a, v = load(ax, 0), load(vx, 0)
    h = halo[pl.ds(pl.multiple_of(jnp.minimum(start_row + size, rows - 8), 8), 8), :]
    beyond = material(a, v, up(a, a), up(v, v), load(rx, 0), load(tx, 0), h)
    nu_next = each(lambda x, y: jnp.where(is_last, pltpu.roll(x, 1, 0), y), cur[0], beyond[0])
    dnu_next = each(lambda x, y: jnp.where(is_last, pltpu.roll(x, 1, 0), y), cur[1], beyond[1])
    fr, dfr = emit(end, cur, halo_at(end), nu_next, dnu_next, fr, dfr)
    for c in range(count):
        cut = slice(c * LANES, (c + 1) * LANES)
        carry_ref[0, :, cut] = fr[c]
        carry_ref[1, :, cut] = dfr[c]


BLOCK = 256


def stencil(potential, direction, source, regions, tables, reg, sat, signs, own, low, high):
    slices, rows, width = potential.shape
    blocks = rows // BLOCK
    whole = pl.BlockSpec((1, BLOCK, width), lambda s, i: (s, i, 0))
    after = pl.BlockSpec(
        (1, 8, width),
        lambda s, i: (s, jnp.minimum((i + 1) * (BLOCK // 8), rows // 8 - 1), 0),
    )
    edge = pl.BlockSpec((1, 8, rows), lambda s, i: (s, 0, 0))
    table = pl.BlockSpec((8, LANES), lambda s, i: (0, 0))
    smem = pl.BlockSpec(memory_space=pltpu.SMEM)
    regv = jnp.broadcast_to(jnp.pad(reg, (0, LANES - NREG)), (8, LANES))
    tabv = jnp.broadcast_to(jnp.pad(sat, (0, LANES - NTAB)), (8, LANES))
    return pl.pallas_call(
        stencil_kernel,
        grid=(slices, blocks),
        in_specs=[smem] * 3 + [table] * 2 + [edge] * 3 + [whole] * 5 + [after] * 4,
        out_specs=[whole, whole],
        out_shape=[jax.ShapeDtypeStruct(potential.shape, jnp.float32)] * 2,
        scratch_shapes=[
            pltpu.VMEM((rows, LANES), jnp.float32),
            pltpu.VMEM((2, 8, width), jnp.float32),
        ],
        compiler_params=pltpu.CompilerParams(vmem_limit_bytes=32 * 2**20),
        cost_estimate=pl.CostEstimate(
            flops=slices * rows * width * 60,
            bytes_accessed=slices * rows * width * 28,
            transcendentals=0,
        ),
    )(
        reg,
        sat,
        signs,
        regv,
        tabv,
        own,
        low,
        high,
        potential,
        direction,
        source,
        regions,
        tables,
        potential,
        direction,
        regions,
        tables,
    )


def gap_kernel(
    azims, mine, rows_ref, w1, tw, w2, w2i, w1i, gains, res_in, jac_in, res_ref, jac_ref, gap_ref,
    grid_z, grid_u, seen_ref,
):
    step = pl.program_id(0)
    devices, slices, _, count, _ = rows_ref.shape
    total = devices // azims * slices
    ka = tw.shape[1]
    own = mine[0]

    def dot(x, y):
        return jnp.dot(x, y, precision=highest, preferred_element_type=jnp.float32)

    @pl.when(step == 0)
    def _():
        owned = 2 * slices
        vectors = owned + 2 * total

        def gather(v, cut, s, q):
            for a in range(azims):
                grid_z[a * count : (a + 1) * count, v * LANES : (v + 1) * LANES] = rows_ref[
                    cut * azims + a, s, q
                ]

        for f in range(2):
            for s in range(slices):
                gather(f * slices + s, own, s, 2 * f)
            for s in range(total):
                gather(owned + f * total + s, s // slices, s % slices, 2 * f + 1)
        first = dot(w1[...], grid_z[...])
        tr, ti = tw[0], tw[1]
        for v in range(vectors):
            re = first[0:ka, v * LANES : (v + 1) * LANES]
            im = first[ka : 2 * ka, v * LANES : (v + 1) * LANES]
            grid_u[v * ka : (v + 1) * ka, 0:LANES] = re * tr - im * ti
            grid_u[v * ka : (v + 1) * ka, LANES : 2 * LANES] = re * ti + im * tr
        bins = dot(grid_u[...], w2[...])

        def part(v):
            return (
                bins[v * ka : (v + 1) * ka, 0:LANES],
                bins[v * ka : (v + 1) * ka, LANES : 2 * LANES],
            )

        k1 = lax.broadcasted_iota(jnp.int32, (ka, LANES), 0)
        k2 = lax.broadcasted_iota(jnp.int32, (ka, LANES), 1)
        freq = 4 * k1 + 4 * ka * k2 + 1
        period = 2 * ka * LANES

        def skew(cut, s):
            offset = jnp.broadcast_to(
                rows_ref[cut * azims, s, 4, 0:1, :].astype(jnp.int32), (ka, LANES)
            )
            angle = (freq * offset & (2 * period - 1)).astype(jnp.float32) * (math.pi / period)
            return jnp.cos(angle), jnp.sin(angle)

        axial = [[0.0, 0.0], [0.0, 0.0]]
        for s in range(total):
            c, d = skew(s // slices, s % slices)
            for f in range(2):
                re, im = part(owned + f * total + s)
                x, y = re * c - im * d, re * d + im * c
                seen_ref[s, f, 0] = x
                seen_ref[s, f, 1] = y
                axial[f][0] = axial[f][0] + x
                axial[f][1] = axial[f][1] + y
        self_gain, cross_gain = gains[0], gains[1]
        for s in range(slices):
            c, d = skew(own, s)
            for f in range(2):
                seen = [seen_ref[own * slices + s, f, i] for i in range(2)]
                rotor = part(f * slices + s)
                blended = [0.5 * (seen[i] + axial[f][i] * (1.0 / total)) for i in range(2)]
                flux = [self_gain * rotor[i] - cross_gain * blended[i] for i in range(2)]
                back = [self_gain * seen[i] - cross_gain * rotor[i] for i in range(2)]
                stator = (back[0] * c + back[1] * d, back[1] * c - back[0] * d)
                for r, value in enumerate((flux, stator)):
                    v = (f * slices + s) * 2 + r
                    grid_u[v * ka : (v + 1) * ka, 0:LANES] = value[0]
                    grid_u[v * ka : (v + 1) * ka, LANES : 2 * LANES] = value[1]
        outs = 4 * slices
        lines = dot(grid_u[0 : outs * ka, :], w2i[...])
        for v in range(outs):
            re = lines[v * ka : (v + 1) * ka, 0:LANES]
            im = lines[v * ka : (v + 1) * ka, LANES : 2 * LANES]
            grid_z[0:ka, v * LANES : (v + 1) * LANES] = re * tr + im * ti
            grid_z[ka : 2 * ka, v * LANES : (v + 1) * LANES] = im * tr - re * ti
        last = dot(w1i[...], grid_z[:, 0 : outs * LANES])
        for f in range(2):
            for s in range(slices):
                for r in range(2):
                    v = (f * slices + s) * 2 + r
                    for c in range(count):
                        gap_ref[f, s, r : r + 1, c * LANES : (c + 1) * LANES] = last[
                            c : c + 1, v * LANES : (v + 1) * LANES
                        ]

    width = res_in.shape[2]
    line = lax.broadcasted_iota(jnp.int32, (8, width), 0)
    for s in range(slices):
        for f, (old, new) in enumerate(((res_in, res_ref), (jac_in, jac_ref))):
            pair = gap_ref[f, s]
            add = jnp.where(step == 0, pair[0:1], pair[1:2])
            target = jnp.where(step == 0, 7, 0)
            new[s] = jnp.where(line == target, old[s] + add, old[s])


def gap(residual, jac_product, gathered, azims, mine, position):
    slices, rows, width = residual.shape
    devices = gathered.shape[0]
    count = width // LANES
    period = azims * width
    ka = period // (2 * LANES)
    w1, tw, w2, w2i, w1i, gains = transform_tables(period)
    lines = -(-count // 8) * 8
    w1i = np.pad(w1i, ((0, lines), (0, 0)))
    mine_w1i = lax.dynamic_slice_in_dim(jnp.asarray(w1i), position * count, lines, 0)
    total = devices // azims * slices
    vectors = 2 * slices + 2 * total
    touched = pl.BlockSpec((slices, 8, width), lambda g: (0, RG // 8 - 1 + g, 0))

    def full(x):
        zeros = (0,) * len(x.shape)
        return pl.BlockSpec(x.shape, lambda g: zeros)

    operands = [gathered] + [jnp.asarray(x) for x in (w1, tw, w2, w2i)]
    operands += [mine_w1i, jnp.asarray(gains)]
    shape = (2, slices, 2, width)
    return pl.pallas_call(
        functools.partial(gap_kernel, azims),
        grid=(2,),
        in_specs=[pl.BlockSpec(memory_space=pltpu.SMEM)]
        + [full(x) for x in operands]
        + [touched, touched],
        out_specs=[touched, touched, pl.BlockSpec(shape, lambda g: (0, 0, 0, 0))],
        out_shape=[
            jax.ShapeDtypeStruct(residual.shape, jnp.float32),
            jax.ShapeDtypeStruct(residual.shape, jnp.float32),
            jax.ShapeDtypeStruct(shape, jnp.float32),
        ],
        scratch_shapes=[
            pltpu.VMEM((2 * ka, vectors * LANES), jnp.float32),
            pltpu.VMEM((vectors * ka, 2 * LANES), jnp.float32),
            pltpu.VMEM((total, 2, 2, ka, LANES), jnp.float32),
        ],
        input_output_aliases={8: 0, 9: 1},
        compiler_params=pltpu.CompilerParams(vmem_limit_bytes=32 * 2**20),
        cost_estimate=pl.CostEstimate(
            flops=vectors * ka * 2 * LANES * 1000, bytes_accessed=2**21, transcendentals=0
        ),
    )(mine, *operands, residual, jac_product)


def body(
    potential, direction, source, region_ids, table_ids, region_reluct, table_sat, skew_offsets
):
    position = lax.axis_index("azim")
    azims = lax.axis_size("azim")
    left, right, rows = edges(potential, direction, region_ids, table_ids, skew_offsets)
    forward = [(i, (i + 1) % azims) for i in range(azims)]
    backward = [(target, source_) for source_, target in forward]
    low = lax.ppermute(right, "azim", forward)
    high = lax.ppermute(left, "azim", backward)
    gathered = lax.all_gather(rows, ("cuts", "azim"))
    signs = jnp.stack(
        [jnp.where(position == 0, -1.0, 1.0), jnp.where(position == azims - 1, -1.0, 1.0)]
    ).astype(jnp.float32)
    residual, jac_product = stencil(
        potential,
        direction,
        source,
        region_ids,
        table_ids,
        region_reluct,
        table_sat,
        signs,
        left,
        low,
        high,
    )
    mine = lax.axis_index("cuts").astype(jnp.int32).reshape(1)
    return tuple(gap(residual, jac_product, gathered, azims, mine, position))


def solution(mesh):
    return jax.shard_map(
        body,
        mesh=mesh,
        in_specs=(
            P("cuts", None, "azim"),
            P("cuts", None, "azim"),
            P("cuts", None, "azim"),
            P("cuts", None, "azim"),
            P("cuts", None, "azim"),
            P(),
            P(),
            P("cuts"),
        ),
        out_specs=(P("cuts", None, "azim"), P("cuts", None, "azim"), P(None, "cuts", None, "azim")),
        check_vma=False,
    )
```

time: 430 us -> 120 us (0.28); the launches traced: 421 us -> 119 us
  other arithmetic: 265 us -> 0.07 us
  local copies, waits for them, and re-layouts: 101 us -> 21.1 us
  Pallas kernels: 0 us -> 49.7 us
  blocking collectives: 16.3 us -> 43.2 us
  matrix products: 16 us -> 0 us
  between operations: 15 us -> 0.72 us
    mul x7 -> x0, other arithmetic: 118 us -> none  [the longest x1 78.5 us: cell_reluct(): dnu_val = 2.0 * base * satur * (rad_p * rad_d + azi_p * azi_d)]
    add x6 -> x0, other arithmetic: 84 us -> none  [the longest x1 61.3 us: cell_fluxes(): return (radial + azim - source, radial_d + azim_d)]
    slice x16 -> x0, local copies, waits for them, and re-layouts: 57.8 us -> none  [the longest x2 18.2 us: neighbours(): jnp.roll(core, -1, axis=-1)]
    pallas_call x0 -> x3, Pallas kernels: none -> 49.7 us  [the longest x1 42.7 us: stencil(): pl.pallas_call(stencil_kernel, grid=(slices, blocks), in_specs=[smem] * 3...]
    all_gather x0 -> x1, blocking collectives: none -> 43.2 us  [body(): gathered = lax.all_gather(rows, ('cuts', 'azim'))]
    sub x4 -> x0, other arithmetic: 37.4 us -> none  [the longest x1 30.9 us: cell_fluxes(): return (radial + azim - source, radial_d + azim_d)]
    cos x2 -> x0, other arithmetic: 16.8 us -> none  [the longest x1 16.5 us: mode_table(): return jnp.concatenate([jnp.cos(phases), jnp.sin(phases)], axis=1)]
    psum x1 -> x0, blocking collectives: 16.3 us -> none  [axial_sum(): return lax.psum(total, 'cuts')]
  transfers between devices with their start and end apart: 5 -> 2, of which waited for: 0 -> 0; matrix products, arithmetic and copies ran while one was open for 82% -> 1% of each run, Pallas kernels for 0% -> 0%
where the time goes in v1:
time: 120 us; the launch traced here: 119 us
  Pallas kernels  49.7 us (41%)
  blocking collectives  43.2 us (36%)
  local copies, waits for them, and re-layouts  21.1 us (18%)
  starting transfers between devices  4.6 us (4%)
    all_gather x1, blocking collectives, body(): gathered = lax.all_gather(rows, ('cuts', 'azim'))  43.2 us
    pallas_call x1, Pallas kernels, stencil(): pl.pallas_call(stencil_kernel, grid=(slices, blocks), in_specs=[smem] * 3...  42.7 us
    unnamed x34, local copies, waits for them, and re-layouts  20.4 us
    ppermute x1, starting transfers between devices, body(): high = lax.ppermute(left, 'azim', backward)  4.1 us
    pallas_call x1, Pallas kernels, edges(): pl.pallas_call(edge_kernel, grid=(slices,), in_specs=[pl.BlockSpec(memory...  3.72 us
    pallas_call x1, Pallas kernels, gap(): pl.pallas_call(functools.partial(gap_kernel, azims), grid=(2,), in_specs=...  3.24 us
  transfers between devices with their start and end apart: 2, of which 0 were waited for; matrix products, arithmetic and copies ran while one was open for 1% of the time, Pallas kernels for 0%

profile of v1, /device:TPU:0, one launch (start us, length us, event | category | flops | bytes accessed | tf_op | source)
XLA Modules:
  0.0 119.3 jit_solution(13059420362131703984)
XLA Ops:
  0.6 0.0 copy-start
  0.6 2.2 %copy-done = f32[2,1024,512]{2,1,0:T(8,128)S(1)} copy-done((f32[2,1024,512]{2,1,0:T(8,128)S(1)}, f32[2,1024,512]{2,1,0:T(8,128)}, u32[]{:S(2)}) %copy-start) | copy-done | bytes 4194328
  2.8 2.2 %copy-done.2 = f32[2,1024,512]{2,1,0:T(8,128)S(1)} copy-done((f32[2,1024,512]{2,1,0:T(8,128)S(1)}, f32[2,1024,512]{2,1,0:T(8,128)}, u32[]{:S(2)}) %copy-start.2) | copy-done | bytes 4194328
  5.0 2.2 %copy-done.4 = s32[2,1024,512]{2,1,0:T(8,128)S(1)} copy-done((s32[2,1024,512]{2,1,0:T(8,128)S(1)}, s32[2,1024,512]{2,1,0:T(8,128)}, u32[]{:S(2)}) %copy-start.4) | copy-done | bytes 4194328
  7.2 2.2 %copy-done.6 = s32[2,1024,512]{2,1,0:T(8,128)S(1)} copy-done((s32[2,1024,512]{2,1,0:T(8,128)S(1)}, s32[2,1024,512]{2,1,0:T(8,128)}, u32[]{:S(2)}) %copy-start.6) | copy-done | bytes 4194328
  9.4 0.7 copy-done.14
  10.0 3.7 %shard_map.157 = (f32[2,8,1024]{2,1,0:T(8,128)S(1)}, f32[2,8,1024]{2,1,0:T(8,128)S(1)}, f32[2,5,4,128]{3,2,1,0:T(4,128)S(1)}) custom-call(s32[2]{0:T(128)S(1)} %copy-done.14, f32[2,1024,512]{2,1,0:T(8,128)S(1)} %copy-done, f32[2,1024,512]{2,1,0:T(8,128)S(1)} %copy-done, f32[2,1024,512]{2,1,0:T(8,128)S(1)} %copy-done.2, f32[2,1024,512]{2,1,0:T(8,128)S(1)} %copy-done.2, ...), custom_call_target="tpu_custom_call" | custom-call | flops 2048000 | bytes 8388608 | tf_op jit(solution)/shard_map/pallas_call | solution.py:93
  13.8 0.5 collective-permute-start
  14.3 4.1 %collective-permute-start.1 = (f32[2,8,1024]{2,1,0:T(8,128)S(1)}, f32[2,8,1024]{2,1,0:T(8,128)S(1)}, u32[]{:S(2)}, u32[]{:S(2)}) collective-permute-start(f32[2,8,1024]{2,1,0:T(8,128)S(1)} %get-tuple-element.9.own_ref), channel_id=1, source_target_pairs={{1,0},{2,1},{3,2},{4,3},{5,4},{6,5},{7,6},{0,7},{9,8},{10,9},{11,1... | collective-permute-start | bytes 196616 | tf_op jit(solution)/shard_map/ppermute | solution.py:568
  18.4 0.0 copy-done.15
  18.4 43.2 %all-gather = f32[64,5,4,128]{3,2,1,0:T(4,128)S(1)} all-gather(f32[2,5,4,128]{3,2,1,0:T(4,128)S(1)} %get-tuple-element.8), channel_id=2, replica_groups=mesh['cuts'=4,'azim'=8] {'cuts','azim'}, dimensions={0}, use_global_device_ids=true | all-gather | bytes 675840 | tf_op jit(solution)/shard_map/all_gather | solution.py:569
  61.6 0.7 constant_dynamic-slice_fusion.w1i
  62.3 0.1 pad_maximum_fusion.sign_s
  62.4 0.0 collective-permute-done.low_ref
  62.4 0.0 collective-permute-done.1.high_ref
  62.4 0.0 copy-start.1
  62.4 2.2 %copy-done.1 = f32[2,1024,512]{2,1,0:T(8,128)S(1)} copy-done((f32[2,1024,512]{2,1,0:T(8,128)S(1)}, f32[2,1024,512]{2,1,0:T(8,128)}, u32[]{:S(2)}) %copy-start.1) | copy-done | bytes 4194328
  64.6 2.2 %copy-done.3 = f32[2,1024,512]{2,1,0:T(8,128)S(1)} copy-done((f32[2,1024,512]{2,1,0:T(8,128)S(1)}, f32[2,1024,512]{2,1,0:T(8,128)}, u32[]{:S(2)}) %copy-start.3) | copy-done | bytes 4194328
  66.8 2.2 %copy-done.5 = s32[2,1024,512]{2,1,0:T(8,128)S(1)} copy-done((s32[2,1024,512]{2,1,0:T(8,128)S(1)}, s32[2,1024,512]{2,1,0:T(8,128)}, u32[]{:S(2)}) %copy-start.5) | copy-done | bytes 4194328
  69.0 2.2 %copy-done.7 = s32[2,1024,512]{2,1,0:T(8,128)S(1)} copy-done((s32[2,1024,512]{2,1,0:T(8,128)S(1)}, s32[2,1024,512]{2,1,0:T(8,128)}, u32[]{:S(2)}) %copy-start.7) | copy-done | bytes 4194328
  71.1 2.2 %copy-done.8 = f32[2,1024,512]{2,1,0:T(8,128)S(1)} copy-done((f32[2,1024,512]{2,1,0:T(8,128)S(1)}, f32[2,1024,512]{2,1,0:T(8,128)}, u32[]{:S(2)}) %copy-start.8) | copy-done | bytes 4194328
  73.3 0.0 copy-start.13
  73.3 42.7 %shard_map.158 = (f32[2,1024,512]{2,1,0:T(8,128)}, f32[2,1024,512]{2,1,0:T(8,128)}) custom-call(f32[8]{0:T(128)S(1)} %copy-done.15, f32[16]{0:T(128)S(1)} %copy-done.16, f32[2]{0:T(128)S(1)} %pad_maximum_fusion.sign_s, f32[8,128]{1,0:T(8,128)S(1)} %broadcast_in_dim.6.regv, f32[8,128]{1,0:T(8,128)S(1)} %broadcast_in_dim.7.tabv, ...), custom_call_target="tpu_custom_call" | custom-call | flops 62914560 | bytes 29360128 | tf_op jit(solution)/shard_map/pallas_call | solution.py:369
  116.1 3.2 %shard_map.159 = (f32[2,1024,512]{2,1,0:T(8,128)}, f32[2,1024,512]{2,1,0:T(8,128)}, f32[2,2,2,512]{3,2,1,0:T(2,128)}) custom-call(s32[1]{0:T(128)} %bitcast.mine, f32[32,2,5,4,128]{4,3,2,1,0:T(4,128)S(1)} %bitcast.4, f32[32,32]{1,0:T(8,128)S(1)} %copy-done.13, f32[2,16,128]{2,1,0:T(8,128)S(1)} %copy-done.12, ...), custom_call_target="tpu_custom_call", output_to_operand_aliasing={{0}: (8, {}), {1}: (9, {})} | custom-call | flops 81920000 | bytes 2097152 | tf_op jit(solution)/shard_map/pallas_call | solution.py:534
  (24 shorter events, 0.0 us)
Async XLA Ops:
  0.6 2.2 %copy-start = (f32[2,1024,512]{2,1,0:T(8,128)S(1)}, f32[2,1024,512]{2,1,0:T(8,128)}, u32[]{:S(2)}) copy-start(f32[2,1024,512]{2,1,0:T(8,128)} %ax.1) | copy-start | bytes 12582916
  2.8 2.2 %copy-start.2 = (f32[2,1024,512]{2,1,0:T(8,128)S(1)}, f32[2,1024,512]{2,1,0:T(8,128)}, u32[]{:S(2)}) copy-start(f32[2,1024,512]{2,1,0:T(8,128)} %vx.1) | copy-start | bytes 12582916
  5.0 2.2 %copy-start.4 = (s32[2,1024,512]{2,1,0:T(8,128)S(1)}, s32[2,1024,512]{2,1,0:T(8,128)}, u32[]{:S(2)}) copy-start(s32[2,1024,512]{2,1,0:T(8,128)} %rx.1) | copy-start | bytes 12582916
  7.2 2.2 %copy-start.6 = (s32[2,1024,512]{2,1,0:T(8,128)S(1)}, s32[2,1024,512]{2,1,0:T(8,128)}, u32[]{:S(2)}) copy-start(s32[2,1024,512]{2,1,0:T(8,128)} %tx.1) | copy-start | bytes 12582916
  9.4 0.7 copy-start.14
  10.0 8.3 %copy-start.15 = (f32[8]{0:T(128)S(1)}, f32[8]{0:T(128)}, u32[]{:S(2)}) copy-start(f32[8]{0:T(128)} %reg_s.1) | copy-start | bytes 100
  10.0 8.3 %copy-start.16 = (f32[16]{0:T(128)S(1)}, f32[16]{0:T(128)}, u32[]{:S(2)}) copy-start(f32[16]{0:T(128)} %tab_s.1) | copy-start | bytes 196
  13.8 48.6 %collective-permute-start = (f32[2,8,1024]{2,1,0:T(8,128)S(1)}, f32[2,8,1024]{2,1,0:T(8,128)S(1)}, u32[]{:S(2)}, u32[]{:S(2)}) collective-permute-start(f32[2,8,1024]{2,1,0:T(8,128)S(1)} %get-tuple-element.10), channel_id=1, source_target_pairs={{0,1},{1,2},{2,3},{3,4},{4,5},{5,6},{6,7},{7,0},{8,9},{9,10},{10,1... | collective-permute-start | bytes 196616 | tf_op jit(solution)/shard_map/ppermute | solution.py:567
  14.3 48.1 %collective-permute-start.1 = (f32[2,8,1024]{2,1,0:T(8,128)S(1)}, f32[2,8,1024]{2,1,0:T(8,128)S(1)}, u32[]{:S(2)}, u32[]{:S(2)}) collective-permute-start(f32[2,8,1024]{2,1,0:T(8,128)S(1)} %get-tuple-element.9.own_ref), channel_id=1, source_target_pairs={{1,0},{2,1},{3,2},{4,3},{5,4},{6,5},{7,6},{0,7},{9,8},{10,9},{11,1... | collective-permute-start | bytes 196616 | tf_op jit(solution)/shard_map/ppermute | solution.py:568
  62.4 2.2 %copy-start.1 = (f32[2,1024,512]{2,1,0:T(8,128)S(1)}, f32[2,1024,512]{2,1,0:T(8,128)}, u32[]{:S(2)}) copy-start(f32[2,1024,512]{2,1,0:T(8,128)} %ax.1) | copy-start | bytes 12582916
  64.6 2.2 %copy-start.3 = (f32[2,1024,512]{2,1,0:T(8,128)S(1)}, f32[2,1024,512]{2,1,0:T(8,128)}, u32[]{:S(2)}) copy-start(f32[2,1024,512]{2,1,0:T(8,128)} %vx.1) | copy-start | bytes 12582916
  66.8 2.2 %copy-start.5 = (s32[2,1024,512]{2,1,0:T(8,128)S(1)}, s32[2,1024,512]{2,1,0:T(8,128)}, u32[]{:S(2)}) copy-start(s32[2,1024,512]{2,1,0:T(8,128)} %rx.1) | copy-start | bytes 12582916
  68.9 2.2 %copy-start.7 = (s32[2,1024,512]{2,1,0:T(8,128)S(1)}, s32[2,1024,512]{2,1,0:T(8,128)}, u32[]{:S(2)}) copy-start(s32[2,1024,512]{2,1,0:T(8,128)} %tx.1) | copy-start | bytes 12582916
  71.1 2.2 %copy-start.8 = (f32[2,1024,512]{2,1,0:T(8,128)S(1)}, f32[2,1024,512]{2,1,0:T(8,128)}, u32[]{:S(2)}) copy-start(f32[2,1024,512]{2,1,0:T(8,128)} %src_ref.1) | copy-start | bytes 12582916
  73.3 42.7 %copy-start.9 = (f32[256,256]{1,0:T(8,128)S(1)}, f32[256,256]{1,0:T(8,128)}, u32[]{:S(2)}) copy-start(f32[256,256]{1,0:T(8,128)} %constant.38.clone.w2i) | copy-start | bytes 786436
  73.3 42.7 %copy-start.10 = (f32[256,256]{1,0:T(8,128)S(1)}, f32[256,256]{1,0:T(8,128)}, u32[]{:S(2)}) copy-start(f32[256,256]{1,0:T(8,128)} %constant.37.clone.w2) | copy-start | bytes 786436
  73.3 42.7 %copy-start.11 = (f32[2,16,128]{2,1,0:T(8,128)S(1)}, f32[2,16,128]{2,1,0:T(8,128)}, u32[]{:S(2)}) copy-start(f32[2,16,128]{2,1,0:T(8,128)} %constant.39.clone.gains) | copy-start | bytes 49156
  73.3 42.7 %copy-start.12 = (f32[2,16,128]{2,1,0:T(8,128)S(1)}, f32[2,16,128]{2,1,0:T(8,128)}, u32[]{:S(2)}) copy-start(f32[2,16,128]{2,1,0:T(8,128)} %constant.36.clone.tw) | copy-start | bytes 49156
  73.3 42.7 %copy-start.13 = (f32[32,32]{1,0:T(8,128)S(1)}, f32[32,32]{1,0:T(8,128)}, u32[]{:S(2)}) copy-start(f32[32,32]{1,0:T(8,128)} %constant.35.clone.w1) | copy-start | bytes 12292

commit v2 on v1

--- a/solution.py
+++ b/solution.py
@@ -106,7 +106,7 @@
             jax.ShapeDtypeStruct((slices, 8, rows), jnp.float32),
             jax.ShapeDtypeStruct((slices, 5, count, LANES), jnp.float32),
         ],
-        compiler_params=pltpu.CompilerParams(vmem_limit_bytes=32 * 2**20),
+        compiler_params=pltpu.CompilerParams(vmem_limit_bytes=58 * 2**20),
         cost_estimate=pl.CostEstimate(
             flops=slices * rows * 1000, bytes_accessed=slices * rows * 4096, transcendentals=0
         ),
@@ -125,6 +125,75 @@
         direction,
         direction,
     )
+
+
+def exchange_kernel(
+    azims, cuts, left, right, rows, low, high, gathered, edge_send, edge_recv, azim_send, azim_recv,
+    cut_send, cut_recv,
+):
+    pos = lax.axis_index("azim")
+    cut = lax.axis_index("cuts")
+    mesh_id = pl.DeviceIdType.MESH
+
+    def along(axis, here, number, k):
+        return {axis: lax.rem(here + k, number)}
+
+    peers = [along("azim", pos, azims, k) for k in range(1, azims)]
+    others = [along("cuts", cut, cuts, k) for k in range(1, cuts)]
+    barrier = pltpu.get_barrier_semaphore()
+    for peer in peers + others:
+        pl.semaphore_signal(barrier, inc=1, device_id=peer, device_id_type=mesh_id)
+    pl.semaphore_wait(barrier, len(peers) + len(others))
+
+    def send(src, dst, send_sem, recv_sem, peer):
+        copy = pltpu.make_async_remote_copy(
+            src_ref=src,
+            dst_ref=dst,
+            send_sem=send_sem,
+            recv_sem=recv_sem,
+            device_id=peer,
+            device_id_type=mesh_id,
+        )
+        copy.start()
+        return copy
+
+    slot = gathered.at[cut, pos]
+    inner = [
+        send(rows, slot, azim_send.at[k], azim_recv.at[k], peer) for k, peer in enumerate(peers)
+    ]
+    borders = [
+        send(right, low, edge_send.at[0], edge_recv.at[0], along("azim", pos, azims, 1)),
+        send(left, high, edge_send.at[1], edge_recv.at[1], along("azim", pos, azims, azims - 1)),
+    ]
+    gathered[cut, pos] = rows[...]
+    for copy in inner:
+        copy.wait()
+    outer = [
+        send(gathered.at[cut], gathered.at[cut], cut_send.at[k], cut_recv.at[k], peer)
+        for k, peer in enumerate(others)
+    ]
+    for copy in borders + outer:
+        copy.wait()
+
+
+def exchange(left, right, rows):
+    azims, cuts = lax.axis_size("azim"), lax.axis_size("cuts")
+    vmem = pl.BlockSpec(memory_space=pltpu.VMEM)
+    dma = pltpu.SemaphoreType.DMA
+    return pl.pallas_call(
+        functools.partial(exchange_kernel, azims, cuts),
+        in_specs=[vmem] * 3,
+        out_specs=[vmem] * 3,
+        out_shape=[
+            jax.ShapeDtypeStruct(left.shape, jnp.float32),
+            jax.ShapeDtypeStruct(left.shape, jnp.float32),
+            jax.ShapeDtypeStruct((cuts, azims) + rows.shape, jnp.float32),
+        ],
+        scratch_shapes=[dma((2,))] * 2 + [dma((azims - 1,))] * 2 + [dma((cuts - 1,))] * 2,
+        compiler_params=pltpu.CompilerParams(
+            collective_id=0, has_side_effects=True, vmem_limit_bytes=58 * 2**20
+        ),
+    )(left, right, rows)
 
 
 def stencil_kernel(
@@ -221,13 +290,13 @@
 
     def up(x, follow):
         return [
-            jnp.where(at_bottom, pltpu.roll(y, 7, 0), pltpu.roll(z, 7, 0))
+            pltpu.roll(jnp.where(at_top, y, z), 7, 0)
             for z, y in zip(x, follow)
         ]
 
     def down(x, before):
         return [
-            jnp.where(at_top, pltpu.roll(y, 1, 0), pltpu.roll(z, 1, 0))
+            pltpu.roll(jnp.where(at_bottom, y, z), 1, 0)
             for z, y in zip(x, before)
         ]
 
@@ -321,7 +390,7 @@
         fr, dfr = emit(at, cur, halo_at(at), following[0], following[1], fr, dfr)
         return following, fr, dfr
 
-    cur, fr, dfr = lax.fori_loop(0, tiles - 2, step, (cur, fr, dfr))
+    cur, fr, dfr = lax.fori_loop(0, tiles - 2, step, (cur, fr, dfr), unroll=3)
 
     is_last = block == blocks - 1
     is_gap = start_row + size == RG
@@ -376,7 +445,7 @@
             pltpu.VMEM((rows, LANES), jnp.float32),
             pltpu.VMEM((2, 8, width), jnp.float32),
         ],
-        compiler_params=pltpu.CompilerParams(vmem_limit_bytes=32 * 2**20),
+        compiler_params=pltpu.CompilerParams(vmem_limit_bytes=58 * 2**20),
         cost_estimate=pl.CostEstimate(
             flops=slices * rows * width * 60,
             bytes_accessed=slices * rows * width * 28,
@@ -549,7 +618,7 @@
             pltpu.VMEM((total, 2, 2, ka, LANES), jnp.float32),
         ],
         input_output_aliases={8: 0, 9: 1},
-        compiler_params=pltpu.CompilerParams(vmem_limit_bytes=32 * 2**20),
+        compiler_params=pltpu.CompilerParams(vmem_limit_bytes=58 * 2**20),
         cost_estimate=pl.CostEstimate(
             flops=vectors * ka * 2 * LANES * 1000, bytes_accessed=2**21, transcendentals=0
         ),
@@ -562,11 +631,8 @@
     position = lax.axis_index("azim")
     azims = lax.axis_size("azim")
     left, right, rows = edges(potential, direction, region_ids, table_ids, skew_offsets)
-    forward = [(i, (i + 1) % azims) for i in range(azims)]
-    backward = [(target, source_) for source_, target in forward]
-    low = lax.ppermute(right, "azim", forward)
-    high = lax.ppermute(left, "azim", backward)
-    gathered = lax.all_gather(rows, ("cuts", "azim"))
+    low, high, gathered = exchange(left, right, rows)
+    gathered = gathered.reshape((-1,) + rows.shape)
     signs = jnp.stack(
         [jnp.where(position == 0, -1.0, 1.0), jnp.where(position == azims - 1, -1.0, 1.0)]
     ).astype(jnp.float32)

time: 120 us -> 69.1 us (0.58)
  blocking collectives: 43.2 us -> 0 us
  local copies, waits for them, and re-layouts: 21.1 us -> 3.79 us
  Pallas kernels: 49.7 us -> 63.7 us
  starting transfers between devices: 4.6 us -> 0 us
    all_gather x1 -> x0, blocking collectives: 43.2 us -> none  [body(): gathered = lax.all_gather(rows, ('cuts', 'azim'))]
    pallas_call x0 -> x1, Pallas kernels: none -> 21.6 us  [exchange(): pl.pallas_call(functools.partial(exchange_kernel, azims, cuts), in_specs=...]
    unnamed x34 -> x0, local copies, waits for them, and re-layouts: 20.4 us -> none
    pallas_call x1, Pallas kernels: 42.7 us -> 32.9 us  [stencil(): pl.pallas_call(stencil_kernel, grid=(slices, blocks), in_specs=[smem] * 3...]
    ppermute x2 -> x0, starting transfers between devices: 4.6 us -> none  [the longest x1 4.1 us: body(): high = lax.ppermute(left, 'azim', backward)]
    pallas_call x1, Pallas kernels: 3.72 us -> 5.46 us  [edges(): pl.pallas_call(edge_kernel, grid=(slices,), in_specs=[pl.BlockSpec(memory...]
  transfers between devices with their start and end apart: 2 -> 0, of which waited for: 0 -> 0; matrix products, arithmetic and copies ran while one was open for 1% -> 0% of each run, Pallas kernels for 0% -> 0%
where the time goes in v2:
time: 69.1 us; the launch traced here: 68.8 us
  Pallas kernels  63.7 us (92%)
  local copies, waits for them, and re-layouts  3.79 us (5%)
    pallas_call x1, Pallas kernels, stencil(): pl.pallas_call(stencil_kernel, grid=(slices, blocks), in_specs=[smem] * 3...  32.9 us
    pallas_call x1, Pallas kernels, exchange(): pl.pallas_call(functools.partial(exchange_kernel, azims, cuts), in_specs=...  21.6 us
    pallas_call x1, Pallas kernels, edges(): pl.pallas_call(edge_kernel, grid=(slices,), in_specs=[pl.BlockSpec(memory...  5.46 us
    pallas_call x1, Pallas kernels, gap(): pl.pallas_call(functools.partial(gap_kernel, azims), grid=(2,), in_specs=...  3.8 us

profile of v2, /device:TPU:0, one launch (start us, length us, event | category | flops | bytes accessed | tf_op | source)
XLA Modules:
  0.0 68.8 jit_solution(3928826134264143335)
XLA Ops:
  0.6 0.6 pad_maximum_fusion.sign_s
  1.3 0.7 pad.8
  1.9 0.7 pad.9
  2.6 0.6 broadcast_in_dim.7.tabv
  3.2 0.6 broadcast_in_dim.6.regv
  3.8 1.3 %constant_dynamic-slice_fusion.w1i = f32[8,32]{1,0:T(8,128)} fusion(f32[40,32]{1,0:T(8,128)} %constant.34.clone, s32[]{:T(128)S(6)} %select_n.10), kind=kLoop, calls=%fused_computation.1 | loop fusion | bytes 2052 | tf_op jit(solution)/shard_map/dynamic_slice | solution.py:591
  5.1 5.5 %shard_map.157 = (f32[2,8,1024]{2,1,0:T(8,128)}, f32[2,8,1024]{2,1,0:T(8,128)}, f32[2,5,4,128]{3,2,1,0:T(4,128)}) custom-call(s32[2]{0:T(128)} %off_ref.1, f32[2,1024,512]{2,1,0:T(8,128)} %ax.1, f32[2,1024,512]{2,1,0:T(8,128)} %ax.1, f32[2,1024,512]{2,1,0:T(8,128)} %vx.1, f32[2,1024,512]{2,1,0:T(8,128)} %vx.1, s32[2,1024,512]{2,1,0:T(8,128)} %rx.1, ...), custom_call_target="tpu_custom_call" | custom-call | flops 2048000 | bytes 8388608 | tf_op jit(solution)/shard_map/pallas_call | solution.py:93
  10.5 21.6 %shard_map.158 = (f32[2,8,1024]{2,1,0:T(8,128)}, f32[2,8,1024]{2,1,0:T(8,128)}, f32[4,8,2,5,4,128]{5,4,3,2,1,0:T(4,128)}) custom-call(f32[2,8,1024]{2,1,0:T(8,128)} %get-tuple-element.11.left.own_ref, f32[2,8,1024]{2,1,0:T(8,128)} %get-tuple-element.12.right, f32[2,5,4,128]{3,2,1,0:T(4,128)} %get-tuple-element.13.rows), custom_call_target="tpu_custom_call" | custom-call | tf_op jit(solution)/shard_map/pallas_call | solution.py:183
  32.1 32.9 %shard_map.159 = (f32[2,1024,512]{2,1,0:T(8,128)}, f32[2,1024,512]{2,1,0:T(8,128)}) custom-call(f32[8]{0:T(128)} %reg_s.1, f32[16]{0:T(128)} %tab_s.1, f32[2]{0:T(128)} %pad_maximum_fusion.sign_s, f32[8,128]{1,0:T(8,128)} %broadcast_in_dim.6.regv, f32[8,128]{1,0:T(8,128)} %broadcast_in_dim.7.tabv, f32[2,8,1024]{2,1,0:T(8,128)} %get-tuple-element.11.left.own_ref, ...), custom_call_target="tpu_custom_call" | custom-call | flops 62914560 | bytes 29360128 | tf_op jit(solution)/shard_map/pallas_call | solution.py:438
  65.0 3.8 %shard_map.160 = (f32[2,1024,512]{2,1,0:T(8,128)}, f32[2,1024,512]{2,1,0:T(8,128)}, f32[2,2,2,512]{3,2,1,0:T(2,128)}) custom-call(s32[1]{0:T(128)} %bitcast.mine, f32[32,2,5,4,128]{4,3,2,1,0:T(4,128)} %bitcast.4, f32[32,32]{1,0:T(8,128)} %constant.35.clone.w1, f32[2,16,128]{2,1,0:T(8,128)} %constant.36.clone.tw, ...), custom_call_target="tpu_custom_call", output_to_operand_aliasing={{0}: (8, {}), {1}: (9, {})} | custom-call | flops 81920000 | bytes 2097152 | tf_op jit(solution)/shard_map/pallas_call | solution.py:603

commit v3 on v2

--- a/solution.py
+++ b/solution.py
@@ -74,11 +74,11 @@
     count = rows_ref.shape[2]
     for c in range(count):
         cut = pl.ds(c * LANES, LANES)
-        rows_ref[0, 0, c : c + 1, :] = a0[0, 7:8, cut]
-        rows_ref[0, 1, c : c + 1, :] = a1[0, 0:1, cut]
-        rows_ref[0, 2, c : c + 1, :] = v0[0, 7:8, cut]
-        rows_ref[0, 3, c : c + 1, :] = v1[0, 0:1, cut]
-        rows_ref[0, 4, c : c + 1, :] = jnp.full((1, LANES), off_ref[s], jnp.int32).astype(
+        rows_ref[3, 0, c : c + 1, :] = a0[0, 7:8, cut]
+        rows_ref[0, 0, c : c + 1, :] = a1[0, 0:1, cut]
+        rows_ref[4, 0, c : c + 1, :] = v0[0, 7:8, cut]
+        rows_ref[1, 0, c : c + 1, :] = v1[0, 0:1, cut]
+        rows_ref[2, 0, c : c + 1, :] = jnp.full((1, LANES), off_ref[s], jnp.int32).astype(
             jnp.float32
         )
 
@@ -99,12 +99,12 @@
         out_specs=[
             pl.BlockSpec((1, 8, rows), lambda s: (s, 0, 0)),
             pl.BlockSpec((1, 8, rows), lambda s: (s, 0, 0)),
-            pl.BlockSpec((1, 5, count, LANES), lambda s: (s, 0, 0, 0)),
+            pl.BlockSpec((5, 1, count, LANES), lambda s: (0, s, 0, 0)),
         ],
         out_shape=[
             jax.ShapeDtypeStruct((slices, 8, rows), jnp.float32),
             jax.ShapeDtypeStruct((slices, 8, rows), jnp.float32),
-            jax.ShapeDtypeStruct((slices, 5, count, LANES), jnp.float32),
+            jax.ShapeDtypeStruct((5, slices, count, LANES), jnp.float32),
         ],
         compiler_params=pltpu.CompilerParams(vmem_limit_bytes=58 * 2**20),
         cost_estimate=pl.CostEstimate(
@@ -168,8 +168,9 @@
     gathered[cut, pos] = rows[...]
     for copy in inner:
         copy.wait()
+    shared = gathered.at[cut, :, 0:3]
     outer = [
-        send(gathered.at[cut], gathered.at[cut], cut_send.at[k], cut_recv.at[k], peer)
+        send(shared, shared, cut_send.at[k], cut_recv.at[k], peer)
         for k, peer in enumerate(others)
     ]
     for copy in borders + outer:
@@ -199,9 +200,6 @@
 def stencil_kernel(
     reg_s,
     tab_s,
-    sign_s,
-    regv,
-    tabv,
     own_ref,
     low_ref,
     high_ref,
@@ -232,8 +230,12 @@
     at_start = lane == 0
     at_bottom = row == 7
     at_top = row == 0
-    reg_tab = jnp.broadcast_to(regv[0:1, :], shape)
-    sat_tab = jnp.broadcast_to(tabv[0:1, :], shape)
+    reg_tab = jnp.zeros(shape, jnp.float32)
+    for i in range(NREG):
+        reg_tab = jnp.where(lane == i, reg_s[i], reg_tab)
+    sat_tab = jnp.zeros(shape, jnp.float32)
+    for i in range(NTAB):
+        sat_tab = jnp.where(lane == i, tab_s[i], sat_tab)
 
     @pl.when(block == 0)
     def _():
@@ -261,7 +263,9 @@
         own = [own_ref[0, i : i + 1, :] for i in range(6)]
         high = [high_ref[0, i : i + 1, :] for i in range(6)]
         low = [low_ref[0, i : i + 1, :] for i in range(4)]
-        ls, rs = sign_s[0], sign_s[1]
+        position = lax.axis_index("azim")
+        ls = jnp.where(position == 0, -1.0, 1.0)
+        rs = jnp.where(position == lax.axis_size("azim") - 1, -1.0, 1.0)
         high = [x * rs for x in high[:4]] + high[4:]
         low = [x * ls for x in low[:2]] + low[2:]
         nu0, dnu0, _, _ = material(*own)
@@ -422,7 +426,7 @@
 BLOCK = 256
 
 
-def stencil(potential, direction, source, regions, tables, reg, sat, signs, own, low, high):
+def stencil(potential, direction, source, regions, tables, reg, sat, own, low, high):
     slices, rows, width = potential.shape
     blocks = rows // BLOCK
     whole = pl.BlockSpec((1, BLOCK, width), lambda s, i: (s, i, 0))
@@ -431,14 +435,11 @@
         lambda s, i: (s, jnp.minimum((i + 1) * (BLOCK // 8), rows // 8 - 1), 0),
     )
     edge = pl.BlockSpec((1, 8, rows), lambda s, i: (s, 0, 0))
-    table = pl.BlockSpec((8, LANES), lambda s, i: (0, 0))
     smem = pl.BlockSpec(memory_space=pltpu.SMEM)
-    regv = jnp.broadcast_to(jnp.pad(reg, (0, LANES - NREG)), (8, LANES))
-    tabv = jnp.broadcast_to(jnp.pad(sat, (0, LANES - NTAB)), (8, LANES))
     return pl.pallas_call(
         stencil_kernel,
         grid=(slices, blocks),
-        in_specs=[smem] * 3 + [table] * 2 + [edge] * 3 + [whole] * 5 + [after] * 4,
+        in_specs=[smem] * 2 + [edge] * 3 + [whole] * 5 + [after] * 4,
         out_specs=[whole, whole],
         out_shape=[jax.ShapeDtypeStruct(potential.shape, jnp.float32)] * 2,
         scratch_shapes=[
@@ -454,9 +455,6 @@
     )(
         reg,
         sat,
-        signs,
-        regv,
-        tabv,
         own,
         low,
         high,
@@ -473,14 +471,14 @@
 
 
 def gap_kernel(
-    azims, mine, rows_ref, w1, tw, w2, w2i, w1i, gains, res_in, jac_in, res_ref, jac_ref, gap_ref,
+    azims, rows_ref, w1, tw, w2, w2i, w1i, gains, res_in, jac_in, res_ref, jac_ref, gap_ref,
     grid_z, grid_u, seen_ref,
 ):
     step = pl.program_id(0)
-    devices, slices, _, count, _ = rows_ref.shape
+    devices, _, slices, count, _ = rows_ref.shape
     total = devices // azims * slices
     ka = tw.shape[1]
-    own = mine[0]
+    own = lax.axis_index("cuts")
 
     def dot(x, y):
         return jnp.dot(x, y, precision=highest, preferred_element_type=jnp.float32)
@@ -493,14 +491,14 @@
         def gather(v, cut, s, q):
             for a in range(azims):
                 grid_z[a * count : (a + 1) * count, v * LANES : (v + 1) * LANES] = rows_ref[
-                    cut * azims + a, s, q
+                    cut * azims + a, q, s
                 ]
 
         for f in range(2):
             for s in range(slices):
-                gather(f * slices + s, own, s, 2 * f)
+                gather(f * slices + s, own, s, 3 + f)
             for s in range(total):
-                gather(owned + f * total + s, s // slices, s % slices, 2 * f + 1)
+                gather(owned + f * total + s, s // slices, s % slices, f)
         first = dot(w1[...], grid_z[...])
         tr, ti = tw[0], tw[1]
         for v in range(vectors):
@@ -523,7 +521,7 @@
 
         def skew(cut, s):
             offset = jnp.broadcast_to(
-                rows_ref[cut * azims, s, 4, 0:1, :].astype(jnp.int32), (ka, LANES)
+                rows_ref[cut * azims, 2, s, 0:1, :].astype(jnp.int32), (ka, LANES)
             )
             angle = (freq * offset & (2 * period - 1)).astype(jnp.float32) * (math.pi / period)
             return jnp.cos(angle), jnp.sin(angle)
@@ -559,7 +557,7 @@
             im = lines[v * ka : (v + 1) * ka, LANES : 2 * LANES]
             grid_z[0:ka, v * LANES : (v + 1) * LANES] = re * tr + im * ti
             grid_z[ka : 2 * ka, v * LANES : (v + 1) * LANES] = im * tr - re * ti
-        last = dot(w1i[...], grid_z[:, 0 : outs * LANES])
+        last = dot(w1i[lax.axis_index("azim")], grid_z[:, 0 : outs * LANES])
         for f in range(2):
             for s in range(slices):
                 for r in range(2):
@@ -579,7 +577,7 @@
             new[s] = jnp.where(line == target, old[s] + add, old[s])
 
 
-def gap(residual, jac_product, gathered, azims, mine, position):
+def gap(residual, jac_product, gathered, azims):
     slices, rows, width = residual.shape
     devices = gathered.shape[0]
     count = width // LANES
@@ -587,8 +585,8 @@
     ka = period // (2 * LANES)
     w1, tw, w2, w2i, w1i, gains = transform_tables(period)
     lines = -(-count // 8) * 8
-    w1i = np.pad(w1i, ((0, lines), (0, 0)))
-    mine_w1i = lax.dynamic_slice_in_dim(jnp.asarray(w1i), position * count, lines, 0)
+    w1i = w1i.reshape(azims, count, 2 * ka)
+    w1i = np.pad(w1i, ((0, 0), (0, lines - count), (0, 0)))
     total = devices // azims * slices
     vectors = 2 * slices + 2 * total
     touched = pl.BlockSpec((slices, 8, width), lambda g: (0, RG // 8 - 1 + g, 0))
@@ -598,14 +596,12 @@
         return pl.BlockSpec(x.shape, lambda g: zeros)
 
     operands = [gathered] + [jnp.asarray(x) for x in (w1, tw, w2, w2i)]
-    operands += [mine_w1i, jnp.asarray(gains)]
+    operands += [jnp.asarray(w1i), jnp.asarray(gains)]
     shape = (2, slices, 2, width)
     return pl.pallas_call(
         functools.partial(gap_kernel, azims),
         grid=(2,),
-        in_specs=[pl.BlockSpec(memory_space=pltpu.SMEM)]
-        + [full(x) for x in operands]
-        + [touched, touched],
+        in_specs=[full(x) for x in operands] + [touched, touched],
         out_specs=[touched, touched, pl.BlockSpec(shape, lambda g: (0, 0, 0, 0))],
         out_shape=[
             jax.ShapeDtypeStruct(residual.shape, jnp.float32),
@@ -617,25 +613,21 @@
             pltpu.VMEM((vectors * ka, 2 * LANES), jnp.float32),
             pltpu.VMEM((total, 2, 2, ka, LANES), jnp.float32),
         ],
-        input_output_aliases={8: 0, 9: 1},
+        input_output_aliases={7: 0, 8: 1},
         compiler_params=pltpu.CompilerParams(vmem_limit_bytes=58 * 2**20),
         cost_estimate=pl.CostEstimate(
             flops=vectors * ka * 2 * LANES * 1000, bytes_accessed=2**21, transcendentals=0
         ),
-    )(mine, *operands, residual, jac_product)
+    )(*operands, residual, jac_product)
 
 
 def body(
     potential, direction, source, region_ids, table_ids, region_reluct, table_sat, skew_offsets
 ):
-    position = lax.axis_index("azim")
     azims = lax.axis_size("azim")
     left, right, rows = edges(potential, direction, region_ids, table_ids, skew_offsets)
     low, high, gathered = exchange(left, right, rows)
     gathered = gathered.reshape((-1,) + rows.shape)
-    signs = jnp.stack(
-        [jnp.where(position == 0, -1.0, 1.0), jnp.where(position == azims - 1, -1.0, 1.0)]
-    ).astype(jnp.float32)
     residual, jac_product = stencil(
         potential,
         direction,
@@ -644,13 +636,11 @@
         table_ids,
         region_reluct,
         table_sat,
-        signs,
         left,
         low,
         high,
     )
-    mine = lax.axis_index("cuts").astype(jnp.int32).reshape(1)
-    return tuple(gap(residual, jac_product, gathered, azims, mine, position))
+    return tuple(gap(residual, jac_product, gathered, azims))
 
 
 def solution(mesh):

time: 69.1 us -> 61.7 us (0.89)
  local copies, waits for them, and re-layouts: 3.79 us -> 0 us
  Pallas kernels: 63.7 us -> 60.9 us
    pallas_call x1, Pallas kernels: 21.6 us -> 18.8 us  [exchange(): pl.pallas_call(functools.partial(exchange_kernel, azims, cuts), in_specs=...]
    pad x2 -> x0, local copies, waits for them, and re-layouts: 1.32 us -> none  [the longest x1 0.66 us: stencil(): regv = jnp.broadcast_to(jnp.pad(reg, (0, LANES - NREG)), (8, LANES))]
    dynamic_slice x1 -> x0, local copies, waits for them, and re-layouts: 1.29 us -> none  [gap(): lax.dynamic_slice_in_dim(jnp.asarray(w1i), position * count, lines, 0)]
    broadcast_in_dim x2 -> x0, local copies, waits for them, and re-layouts: 1.18 us -> none  [the longest x1 0.59 us: stencil(): regv = jnp.broadcast_to(jnp.pad(reg, (0, LANES - NREG)), (8, LANES))]
where the time goes in v3:
time: 61.7 us; the launch traced here: 61.6 us
  Pallas kernels  60.9 us (99%)
  between operations  0.64 us (1%)
    pallas_call x1, Pallas kernels, stencil(): pl.pallas_call(stencil_kernel, grid=(slices, blocks), in_specs=[smem] * 2...  32.8 us
    pallas_call x1, Pallas kernels, exchange(): pl.pallas_call(functools.partial(exchange_kernel, azims, cuts), in_specs=...  18.8 us
    pallas_call x1, Pallas kernels, edges(): pl.pallas_call(edge_kernel, grid=(slices,), in_specs=[pl.BlockSpec(memory...  5.49 us
    pallas_call x1, Pallas kernels, gap(): pl.pallas_call(functools.partial(gap_kernel, azims), grid=(2,), in_specs=...  3.81 us

profile of v3, /device:TPU:0, one launch (start us, length us, event | category | flops | bytes accessed | tf_op | source)
XLA Modules:
  0.0 61.6 jit_solution(15361235612139217614)
XLA Ops:
  0.6 5.5 %shard_map.157 = (f32[2,8,1024]{2,1,0:T(8,128)}, f32[2,8,1024]{2,1,0:T(8,128)}, f32[5,2,4,128]{3,2,1,0:T(4,128)}) custom-call(s32[2]{0:T(128)} %off_ref.1, f32[2,1024,512]{2,1,0:T(8,128)} %ax.1, f32[2,1024,512]{2,1,0:T(8,128)} %ax.1, f32[2,1024,512]{2,1,0:T(8,128)} %vx.1, f32[2,1024,512]{2,1,0:T(8,128)} %vx.1, s32[2,1024,512]{2,1,0:T(8,128)} %rx.1, ...), custom_call_target="tpu_custom_call" | custom-call | flops 2048000 | bytes 8388608 | tf_op jit(solution)/shard_map/pallas_call | solution.py:93
  6.1 18.8 %shard_map.158 = (f32[2,8,1024]{2,1,0:T(8,128)}, f32[2,8,1024]{2,1,0:T(8,128)}, f32[4,8,5,2,4,128]{5,4,3,2,1,0:T(4,128)}) custom-call(f32[2,8,1024]{2,1,0:T(8,128)} %get-tuple-element.11.left.own_ref, f32[2,8,1024]{2,1,0:T(8,128)} %get-tuple-element.12.right, f32[5,2,4,128]{3,2,1,0:T(4,128)} %get-tuple-element.13.rows), custom_call_target="tpu_custom_call" | custom-call | tf_op jit(solution)/shard_map/pallas_call | solution.py:184
  24.9 32.8 %shard_map.159 = (f32[2,1024,512]{2,1,0:T(8,128)}, f32[2,1024,512]{2,1,0:T(8,128)}) custom-call(f32[8]{0:T(128)} %reg_s.1, f32[16]{0:T(128)} %tab_s.1, f32[2,8,1024]{2,1,0:T(8,128)} %get-tuple-element.11.left.own_ref, f32[2,8,1024]{2,1,0:T(8,128)} %get-tuple-element.15.low_ref, f32[2,8,1024]{2,1,0:T(8,128)} %get-tuple-element.16.high_ref, ...), custom_call_target="tpu_custom_call" | custom-call | flops 62914560 | bytes 29360128 | tf_op jit(solution)/shard_map/pallas_call | solution.py:439
  57.7 3.8 %shard_map.160 = (f32[2,1024,512]{2,1,0:T(8,128)}, f32[2,1024,512]{2,1,0:T(8,128)}, f32[2,2,2,512]{3,2,1,0:T(2,128)}) custom-call(f32[32,5,2,4,128]{4,3,2,1,0:T(4,128)} %bitcast.1, f32[32,32]{1,0:T(8,128)} %constant.12.clone.w1, f32[2,16,128]{2,1,0:T(8,128)} %constant.13.clone.tw, ...), custom_call_target="tpu_custom_call", output_to_operand_aliasing={{0}: (7, {}), {1}: (8, {})} | custom-call | flops 81920000 | bytes 2097152 | tf_op jit(solution)/shard_map/pallas_call | solution.py:601
